TPU v7x, 128 devices: a whole 4x4x4 slice. The times are simulated.
128 devices in a mesh: dp: 16 (over z, x_lo, core), fsdp: 8 (over y, x_hi).
Axes of the slice: x: 4 (x_hi: 2, x_lo: 2; x = x_hi * 2 + x_lo), y: 4, z: 4, core: 2. Of those that a mesh axis runs over, the one named last changes fastest.
Arguments:
- images: bfloat16 [256, 8, 8, 3072], P(('dp', 'fsdp')), may hold values from -6 to 6
- grad_out: bfloat16 [256, 8, 8, 3072], P(('dp', 'fsdp')), may hold values from -6 to 6
- dw_weight: float32 [7, 7, 3072], replicated, may hold values from -0.875 to 0.875
- dw_bias: float32 [3072], replicated, may hold values from -3 to 3
- ln_gain: float32 [3072], replicated, may hold values from 0.1 to 1.9
- ln_bias: float32 [3072], replicated, may hold values from -2 to 2
- w_up: bfloat16 [3072, 6144], P(None, 'fsdp'), may hold values from -0.109375 to 0.109375
- b_up: float32 [6144], P('fsdp'), may hold values from -3 to 3
- w_down: bfloat16 [6144, 3072], P('fsdp'), may hold values from -0.15625 to 0.15625
- b_down: float32 [3072], replicated, may hold values from -3 to 3
- layer_scale: float32 [3072], replicated, may hold values from 0.3 to 1.5
Outputs:
- out_images: bfloat16 [256, 8, 8, 3072], P(('dp', 'fsdp'))
- grad_images: bfloat16 [256, 8, 8, 3072], P(('dp', 'fsdp'))
- grad_w_up: bfloat16 [3072, 6144], P(None, 'fsdp')
- grad_b_up: bfloat16 [6144], P('fsdp')
- grad_w_down: bfloat16 [6144, 3072], P('fsdp')
- grad_dw_weight: float32 [7, 7, 3072], replicated
- grad_dw_bias: float32 [3072], replicated
- grad_ln_gain: float32 [3072], replicated
- grad_ln_bias: float32 [3072], replicated
- grad_b_down: float32 [3072], replicated
- grad_layer_scale: float32 [3072], replicated
All inputs are finite; a program needn't handle non-finite values.
Results may differ from a plain program's by a relative error of at most 0.025.
Values may be sent and summed in bfloat16 or wider, within the bound.
A program may use at most 256 MiB of HBM per device.

v0:
```python
import math

import jax
import jax.numpy as jnp
from jax import lax
from jax.sharding import PartitionSpec as P


def depthwise(pixels, kernel, offset):
    margin = kernel.shape[0] // 2
    extent = pixels.shape[1]
    padded = jnp.pad(pixels, ((0, 0), (margin, margin), (margin, margin), (0, 0)))
    summed = jnp.zeros(pixels.shape, jnp.float32)
    for vertical in range(kernel.shape[0]):
        for horizontal in range(kernel.shape[1]):
            summed = (
                summed
                + padded[:, vertical : vertical + extent, horizontal : horizontal + extent, :]
                * kernel[vertical, horizontal]
            )
    return summed + offset


def layer_norm(before_norm, gain, offset):
    average = jnp.mean(before_norm, axis=-1, keepdims=True)
    centred = before_norm - average
    inv_std = lax.rsqrt(jnp.mean(centred * centred, axis=-1, keepdims=True) + 1e-06)
    standard = centred * inv_std
    return (standard * gain + offset, standard, inv_std)


def norm_back(grad_normed, standard, inv_std, gain):
    grad_hat = grad_normed * gain
    centred_grad = (
        grad_hat
        - jnp.mean(grad_hat, axis=-1, keepdims=True)
        - standard * jnp.mean(grad_hat * standard, axis=-1, keepdims=True)
    )
    return (
        inv_std * centred_grad,
        jnp.sum(grad_normed * standard, axis=(0, 1, 2)),
        jnp.sum(grad_normed, axis=(0, 1, 2)),
    )


def gelu_exact(values):
    return 0.5 * values * (1.0 + lax.erf(values * 0.7071067811865476))


def gelu_slope(values):
    return (
        0.5 * (1.0 + lax.erf(values * 0.7071067811865476))
        + values * jnp.exp(-0.5 * values * values) * 0.3989422804014327
    )


def on_device(
    images, grad_out, dw_weight, dw_bias, ln_gain, ln_bias, w_up, b_up, w_down, b_down, layer_scale
):
    channels = images.shape[3]
    local_rows = images.shape[0] * images.shape[1] * images.shape[2]
    pixels = images.astype(jnp.float32)
    upstream = grad_out.astype(jnp.float32)
    before_norm = depthwise(pixels, dw_weight, dw_bias)
    normed_full, standard, inv_std = layer_norm(before_norm, ln_gain, ln_bias)
    normed = normed_full.reshape(local_rows, channels).astype(jnp.bfloat16)
    group_normed = lax.all_gather(normed, "fsdp", axis=0, tiled=True)
    pre_up = jnp.dot(group_normed, w_up, preferred_element_type=jnp.float32) + b_up
    hidden = gelu_exact(pre_up).astype(jnp.bfloat16)
    branch_flat = (
        lax.psum_scatter(
            jnp.dot(hidden, w_down, preferred_element_type=jnp.float32).astype(jnp.bfloat16),
            "fsdp",
            scatter_dimension=0,
            tiled=True,
        ).astype(jnp.float32)
        + b_down
    )
    branch = branch_flat.reshape(images.shape)
    out_images = (pixels + layer_scale * branch).astype(jnp.bfloat16)
    scaled = (layer_scale * upstream).reshape(local_rows, channels).astype(jnp.bfloat16)
    group_scaled = lax.all_gather(scaled, "fsdp", axis=0, tiled=True)
    grad_hidden = lax.dot_general(
        group_scaled, w_down, (((1,), (1,)), ((), ())), preferred_element_type=jnp.float32
    )
    part_down = lax.dot_general(
        hidden, group_scaled, (((0,), (0,)), ((), ())), preferred_element_type=jnp.float32
    )
    grad_pre = (grad_hidden * gelu_slope(pre_up)).astype(jnp.bfloat16)
    part_bias = jnp.sum(grad_pre, axis=0, dtype=jnp.float32)
    part_up = lax.dot_general(
        group_normed, grad_pre, (((0,), (0,)), ((), ())), preferred_element_type=jnp.float32
    )
    grad_normed = (
        lax.psum_scatter(
            lax.dot_general(
                grad_pre, w_up, (((1,), (1,)), ((), ())), preferred_element_type=jnp.float32
            ).astype(jnp.bfloat16),
            "fsdp",
            scatter_dimension=0,
            tiled=True,
        )
        .astype(jnp.float32)
        .reshape(images.shape)
    )
    grad_conv, grad_gain, grad_shift = norm_back(grad_normed, standard, inv_std, ln_gain)
    unused, pullback = jax.vjp(depthwise, pixels, dw_weight, dw_bias)
    grad_pixels, grad_kernel, grad_conv_bias = pullback(grad_conv)
    grad_images = (upstream + grad_pixels).astype(jnp.bfloat16)
    grad_down_bias = jnp.sum(scaled, axis=0, dtype=jnp.float32)
    grad_scale = jnp.sum(upstream * branch, axis=(0, 1, 2))
    factor = 1.0 / math.sqrt(local_rows * lax.axis_size("dp") * lax.axis_size("fsdp"))
    small_sums = lax.psum(
        (grad_kernel, grad_conv_bias, grad_gain, grad_shift, grad_down_bias, grad_scale),
        ("dp", "fsdp"),
    )
    summed_up, summed_down, summed_bias = (
        lax.psum(part_up.astype(jnp.bfloat16), "dp").astype(jnp.float32),
        lax.psum(part_down.astype(jnp.bfloat16), "dp").astype(jnp.float32),
        lax.psum(part_bias.astype(jnp.bfloat16), "dp").astype(jnp.float32),
    )
    grad_w_up = (summed_up * factor).astype(jnp.bfloat16)
    grad_w_down = (summed_down * factor).astype(jnp.bfloat16)
    grad_b_up = (summed_bias * factor).astype(jnp.bfloat16)
    return (
        out_images,
        grad_images,
        grad_w_up,
        grad_b_up,
        grad_w_down,
        small_sums[0] * factor,
        small_sums[1] * factor,
        small_sums[2] * factor,
        small_sums[3] * factor,
        small_sums[4] * factor,
        small_sums[5] * factor,
    )


def solution(mesh):
    return jax.shard_map(
        on_device,
        mesh=mesh,
        in_specs=(
            P(("dp", "fsdp"), None, None, None),
            P(("dp", "fsdp"), None, None, None),
            P(),
            P(),
            P(),
            P(),
            P(None, "fsdp"),
            P("fsdp"),
            P("fsdp", None),
            P(),
            P(),
        ),
        out_specs=(
            P(("dp", "fsdp"), None, None, None),
            P(("dp", "fsdp"), None, None, None),
            P(None, "fsdp"),
            P("fsdp"),
            P("fsdp", None),
            P(),
            P(),
            P(),
            P(),
            P(),
            P(),
        ),
        check_vma=False,
    )
```

profile of v0, /device:TPU:1, one launch (start us, length us, event | category | flops | bytes accessed | tf_op | source)
XLA Modules:
  0.0 870.4 jit_solution(12215808634039628885)
XLA Ops:
  7.2 1.5 fusion.14
  8.8 2.2 fusion.12
  11.1 2.0 fusion.13
  13.2 0.1 convert_element_type.77
  13.4 0.4 copy-done.6
  13.8 13.7 %fusion.11 = (f32[2,8,8]{2,1,0:T(8,128)S(1)}, f32[2,8,8,3072]{3,2,1,0:T(8,128)S(1)}) fusion(f32[3072]{0:T(1024)S(1)} %copy-done.48, f32[3072]{0:T(1024)S(1)} %bitcast.139, f32[3072]{0:T(1024)S(1)} %bitcast.141, f32[3072]{0:T(1024)S(1)} %bitcast.193, f32[3072]{0:T(1024)S(1)} %bitcast.195, f32[3072]{0:T(1024)S(1)} %bitcast.197, f32[3072]{0:T(1024)S(1)} %bitcast.199, ...), kind=kLoop, calls=%fused_computation.199 | loop fusion | flops 39321472 | bytes 4547072 | tf_op jit(solution)/shard_map/reduce_sum | solution.py:25
  27.6 0.3 multiply_reduce_fusion.52
  27.9 0.4 copy-done.5
  28.3 1.2 add_convert_fusion.1
  29.5 0.0 reduce-scatter.3.cloned.1.call-start
  29.6 91.7 %all-gather.3.cloned.1.call-done = bf16[1024,3072]{1,0:T(8,128)(2,1)} async-done(((bf16[128,3072]{1,0:T(8,128)(2,1)}), bf16[1024,3072]{1,0:T(8,128)(2,1)}) %all-gather.3.cloned.1.call-update) | async-done | bytes 6291472 | tf_op jit(solution)/shard_map/all_gather | solution.py:67
  121.3 8.5 fusion.16
  129.8 1.7 copy-done.53
  131.5 9.3 %convolution_convert_fusion.1 = bf16[1024,3072]{1,0:T(8,128)(2,1)} fusion(bf16[768,3072]{1,0:T(8,128)(2,1)} %param.19, f32[1024,768]{1,0:T(8,128)S(1)} %fusion.16, f32[768]{0:T(1024)S(1)} %copy-done.51), kind=kOutput, calls=%fused_computation.51 | convolution fusion | flops 4839702528 | bytes 14158848 | tf_op jit(solution)/shard_map/dot_general | solution.py:72
  140.8 96.0 %reduce-scatter.3.cloned.1.call-done = bf16[128,3072]{1,0:T(8,128)(2,1)} async-done(((bf16[1024,3072]{1,0:T(8,128)(2,1)}), bf16[128,3072]{1,0:T(8,128)(2,1)}) %reduce-scatter.3.cloned.1.call-update) | async-done | bytes 786448 | tf_op jit(solution)/shard_map/reduce_scatter | solution.py:71
  236.8 3.9 convert_reduce_fusion
  240.7 0.2 all-reduce.106.cloned.1.call-start
  240.9 87.3 %all-gather.5.cloned.1.call-done = bf16[1024,3072]{1,0:T(8,128)(2,1)} async-done(((bf16[128,3072]{1,0:T(8,128)(2,1)}), bf16[1024,3072]{1,0:T(8,128)(2,1)}) %all-gather.5.cloned.1.call-update) | async-done | bytes 6291472 | tf_op jit(solution)/shard_map/all_gather | solution.py:82
  328.3 10.6 %fusion.15 = (bf16[768]{0:T(1024)(128)(2,1)}, bf16[1024,768]{1,0:T(8,128)(2,1)S(1)}) fusion(f32[1024,768]{1,0:T(8,128)} %copy-done.53, f32[768]{0:T(1024)} %param.18, bf16[1024,3072]{1,0:T(8,128)(2,1)} %all-gather.5.cloned.1.call-done, bf16[768,3072]{1,0:T(8,128)(2,1)} %param.19), kind=kOutput, calls=%fused_computation.203 | convolution fusion | flops 4841274368 | bytes 15733248 | tf_op jit(solution)/shard_map/dot_general | solution.py:83
  338.9 7.2 convolution_convert_fusion.2
  346.1 9.6 %convolution_convert_fusion.3 = bf16[3072,768]{1,0:T(8,128)(2,1)} fusion(bf16[1024,3072]{1,0:T(8,128)(2,1)} %all-gather.3.cloned.1.call-done, bf16[1024,768]{1,0:T(8,128)(2,1)S(1)} %get-tuple-element.191), kind=kOutput, calls=%fused_computation.54 | convolution fusion | flops 4834197504 | bytes 12582912 | tf_op jit(solution)/shard_map/dot_general | solution.py:91
  355.8 0.0 reduce-scatter.5.cloned.1.call-start
  355.8 9.1 %convolution_convert_fusion = bf16[1024,3072]{1,0:T(8,128)(2,1)} fusion(bf16[1024,768]{1,0:T(8,128)(2,1)} %copy-done.55, bf16[3072,768]{1,0:T(8,128)(2,1)} %param.17), kind=kOutput, calls=%fused_computation.50 | convolution fusion | flops 4834983936 | bytes 12582912 | tf_op jit(solution)/shard_map/dot_general | solution.py:96
  365.0 30.1 %psum.64 = bf16[768]{0:T(1024)(128)(2,1)} all-reduce(bf16[768]{0:T(1024)(128)(2,1)} %get-tuple-element.190), channel_id=1, replica_groups=mesh['dp'=16,'fsdp'=8] {'dp'}, use_global_device_ids=true, to_apply=%region_8.9 | all-reduce | flops 768 | bytes 3072 | tf_op jit(solution)/shard_map/psum | solution.py:120
  395.1 1.3 multiply_convert_fusion.3
  396.4 173.6 %all-reduce.106.cloned.1.call-done = (bf16[3072,768]{1,0:T(8,128)(2,1)}, bf16[768,3072]{1,0:T(8,128)(2,1)}) async-done(((bf16[3072,768]{1,0:T(8,128)(2,1)}, bf16[768,3072]{1,0:T(8,128)(2,1)}), (bf16[3072,768]{1,0:T(8,128)(2,1)}, bf16[768,3072]{1,0:T(8,128)(2,1)})) %all-reduce.106.cloned.1.call-update) | async-done | bytes 9437200 | tf_op jit(solution)/shard_map/psum | solution.py:118
  570.0 5.6 multiply_convert_fusion.1
  575.6 3.3 multiply_convert_fusion
  578.9 93.1 %reduce-scatter.5.cloned.1.call-done = bf16[128,3072]{1,0:T(8,128)(2,1)} async-done(((bf16[1024,3072]{1,0:T(8,128)(2,1)}), bf16[128,3072]{1,0:T(8,128)(2,1)}) %reduce-scatter.5.cloned.1.call-update) | async-done | bytes 786448 | tf_op jit(solution)/shard_map/reduce_scatter | solution.py:95
  672.0 2.0 convert_reduce_fusion.1
  674.0 0.5 broadcast_multiply_fusion.57
  674.5 1.3 div.17
  675.9 2.8 multiply_reduce_fusion
  678.7 3.7 fusion.9
  682.4 3.7 multiply_reduce_fusion.48
  686.2 3.3 multiply_reduce_fusion.49
  689.7 6.0 broadcast_multiply_fusion.2
  695.8 9.6 %broadcast_multiply_fusion.1 = (f32[2,8,8,3072]{3,2,1,0:T(8,128)}, f32[2,8,8,3072]{3,2,1,0:T(8,128)}, f32[2,8,8,3072]{3,2,1,0:T(8,128)}, f32[2,8,8,3072]{3,2,1,0...) fusion(f32[2,8,8,3072]{3,2,1,0:T(8,128)S(1)} %get-tuple-element, ...), kind=kLoop, calls=%fused_computation.138 | loop fusion | flops 7077888 | bytes 30105600 | tf_op jit(solution)/shard_map/transpose(jvp())/mul | solution.py:18
  705.4 9.5 %broadcast_multiply_fusion = (f32[2,8,8,3072]{3,2,1,0:T(8,128)}, f32[2,8,8,3072]{3,2,1,0:T(8,128)}, f32[2,8,8,3072]{3,2,1,0:T(8,128)}, f32[2,8,8,3072]{3,2,1,0:T...) fusion(f32[2,8,8,3072]{3,2,1,0:T(8,128)S(1)} %get-tuple-element, ...), kind=kLoop, calls=%fused_computation.137 | loop fusion | flops 7077888 | bytes 30105600 | tf_op jit(solution)/shard_map/transpose(jvp())/mul | solution.py:18
  714.9 1.8 pad_add_fusion.7
  716.7 28.3 %pad_add_fusion = f32[2,14,14,3072]{3,2,1,0:T(8,128)} fusion(f32[2,8,8,3072]{3,2,1,0:T(8,128)} %get-tuple-element.96, f32[2,8,8,3072]{3,2,1,0:T(8,128)} %get-tuple-element.97, f32[2,8,8,3072]{3,2,1,0:T(8,128)} %get-tuple-element.98, f32[2,8,8,3072]{3,2,1,0:T(8,128)} %get-tuple-element.99, f32[2,8,8,3072]{3,2,1,0:T(8,128)} %get-tuple-element.100, ...), kind=kLoop, calls=%fused_computation.52 | loop fusion | flops 50577408 | bytes 72450048 | tf_op jit(solution)/shard_map/transpose(jvp())/add_any | solution.py:18
  745.1 6.3 fusion.8
  751.4 65.4 %all-reduce.99 = (f32[3072]{0:T(1024)S(1)}, f32[3072]{0:T(1024)S(1)}, f32[3072]{0:T(1024)S(1)}, f32[3072]{0:T(1024)S(1)}, f32[3072]{0:T(1024)S(1)}) all-reduce(f32[3072]{0:T(1024)S(1)} %copy-done.46, f32[3072]{0:T(1024)S(1)} %copy-done.44, f32[3072]{0:T(1024)S(1)} %copy-done.45, ...), channel_id=1, replica_groups=mesh['dp'=16,'fsdp'=8] {'dp','fsdp'}, use_global_device_ids=true, to_apply=%region_61.62 | all-reduce | flops 15360 | bytes 122880 | tf_op jit(solution)/shard_map/psum | solution.py:113
  816.9 0.6 broadcast_multiply_fusion.52
  817.5 0.6 broadcast_multiply_fusion.54
  818.1 0.6 broadcast_multiply_fusion.50
  818.7 42.8 %all-reduce.104.cloned.1.call-done = f32[7,7,3072]{2,1,0:T(8,128)} async-done(((f32[7,7,3072]{2,1,0:T(8,128)}), f32[7,7,3072]{2,1,0:T(8,128)}) %all-reduce.104.cloned.1.call-update) | async-done | bytes 602128 | tf_op jit(solution)/shard_map/psum | solution.py:113
  861.5 2.0 broadcast_multiply_fusion.49
  (121 shorter events, 0.5 us)
Async XLA Ops:
  7.2 6.0 copy-start.1
  7.2 114.1 %all-gather.3.cloned.1.call-start = ((), (), s32[]{:S(2)}) async-start(), calls=%async_computation.2 | async-start | bytes 7077888 | tf_op jit(solution)/shard_map/all_gather | solution.py:67
  11.0 16.4 %copy-start.16 = (f32[1,1,3072]{2,1,0:T(1,128)}, f32[1,1,3072]{2,1,0:T(1,128)S(1)}, u32[]{:S(2)}) copy-start(f32[1,1,3072]{2,1,0:T(1,128)S(1)} %get-tuple-element.141) | copy-start | bytes 36868
  11.0 16.4 %copy-start.18 = (f32[1,1,3072]{2,1,0:T(1,128)}, f32[1,1,3072]{2,1,0:T(1,128)S(1)}, u32[]{:S(2)}) copy-start(f32[1,1,3072]{2,1,0:T(1,128)S(1)} %get-tuple-element.142) | copy-start | bytes 36868
  11.0 16.4 %copy-start.20 = (f32[1,1,3072]{2,1,0:T(1,128)}, f32[1,1,3072]{2,1,0:T(1,128)S(1)}, u32[]{:S(2)}) copy-start(f32[1,1,3072]{2,1,0:T(1,128)S(1)} %get-tuple-element.143) | copy-start | bytes 36868
  11.0 16.4 %copy-start.22 = (f32[1,1,3072]{2,1,0:T(1,128)}, f32[1,1,3072]{2,1,0:T(1,128)S(1)}, u32[]{:S(2)}) copy-start(f32[1,1,3072]{2,1,0:T(1,128)S(1)} %get-tuple-element.144) | copy-start | bytes 36868
  11.0 16.4 %copy-start.24 = (f32[1,1,3072]{2,1,0:T(1,128)}, f32[1,1,3072]{2,1,0:T(1,128)S(1)}, u32[]{:S(2)}) copy-start(f32[1,1,3072]{2,1,0:T(1,128)S(1)} %get-tuple-element.145) | copy-start | bytes 36868
  11.0 16.4 %copy-start.26 = (f32[1,1,3072]{2,1,0:T(1,128)}, f32[1,1,3072]{2,1,0:T(1,128)S(1)}, u32[]{:S(2)}) copy-start(f32[1,1,3072]{2,1,0:T(1,128)S(1)} %get-tuple-element.146) | copy-start | bytes 36868
  11.1 16.4 %copy-start.28 = (f32[1,1,3072]{2,1,0:T(1,128)}, f32[1,1,3072]{2,1,0:T(1,128)S(1)}, u32[]{:S(2)}) copy-start(f32[1,1,3072]{2,1,0:T(1,128)S(1)} %get-tuple-element.147) | copy-start | bytes 36868
  11.1 16.4 %copy-start.30 = (f32[1,1,3072]{2,1,0:T(1,128)}, f32[1,1,3072]{2,1,0:T(1,128)S(1)}, u32[]{:S(2)}) copy-start(f32[1,1,3072]{2,1,0:T(1,128)S(1)} %get-tuple-element.148) | copy-start | bytes 36868
  11.1 16.4 %copy-start.32 = (f32[1,1,3072]{2,1,0:T(1,128)}, f32[1,1,3072]{2,1,0:T(1,128)S(1)}, u32[]{:S(2)}) copy-start(f32[1,1,3072]{2,1,0:T(1,128)S(1)} %get-tuple-element.149) | copy-start | bytes 36868
  11.1 16.4 %copy-start.34 = (f32[1,1,3072]{2,1,0:T(1,128)}, f32[1,1,3072]{2,1,0:T(1,128)S(1)}, u32[]{:S(2)}) copy-start(f32[1,1,3072]{2,1,0:T(1,128)S(1)} %get-tuple-element.150) | copy-start | bytes 36868
  11.1 16.4 %copy-start.36 = (f32[1,1,3072]{2,1,0:T(1,128)}, f32[1,1,3072]{2,1,0:T(1,128)S(1)}, u32[]{:S(2)}) copy-start(f32[1,1,3072]{2,1,0:T(1,128)S(1)} %get-tuple-element.151) | copy-start | bytes 36868
  11.1 16.4 %copy-start.38 = (f32[1,1,3072]{2,1,0:T(1,128)}, f32[1,1,3072]{2,1,0:T(1,128)S(1)}, u32[]{:S(2)}) copy-start(f32[1,1,3072]{2,1,0:T(1,128)S(1)} %get-tuple-element.152) | copy-start | bytes 36868
  11.1 16.4 %copy-start.40 = (f32[1,1,3072]{2,1,0:T(1,128)}, f32[1,1,3072]{2,1,0:T(1,128)S(1)}, u32[]{:S(2)}) copy-start(f32[1,1,3072]{2,1,0:T(1,128)S(1)} %get-tuple-element.153) | copy-start | bytes 36868
  13.2 14.4 %copy-start.10 = (f32[1,1,3072]{2,1,0:T(1,128)}, f32[1,1,3072]{2,1,0:T(1,128)S(1)}, u32[]{:S(2)}) copy-start(f32[1,1,3072]{2,1,0:T(1,128)S(1)} %get-tuple-element.169) | copy-start | bytes 36868
  13.2 14.4 %copy-start.12 = (f32[1,1,3072]{2,1,0:T(1,128)}, f32[1,1,3072]{2,1,0:T(1,128)S(1)}, u32[]{:S(2)}) copy-start(f32[1,1,3072]{2,1,0:T(1,128)S(1)} %get-tuple-element.170) | copy-start | bytes 36868
  13.2 14.4 %copy-start.14 = (f32[1,1,3072]{2,1,0:T(1,128)}, f32[1,1,3072]{2,1,0:T(1,128)S(1)}, u32[]{:S(2)}) copy-start(f32[1,1,3072]{2,1,0:T(1,128)S(1)} %get-tuple-element.171) | copy-start | bytes 36868
  29.5 207.3 %reduce-scatter.3.cloned.1.call-start = ((), (), s32[]{:S(2)}) async-start(), calls=%async_computation.3 | async-start | bytes 7077888 | tf_op jit(solution)/shard_map/reduce_scatter | solution.py:71
  121.3 10.2 %copy-start.51 = (f32[768]{0:T(1024)S(1)}, f32[768]{0:T(1024)}, u32[]{:S(2)}) copy-start(f32[768]{0:T(1024)} %param.18) | copy-start | bytes 9220
  140.8 187.5 %all-gather.5.cloned.1.call-start = ((), (), s32[]{:S(2)}) async-start(), calls=%async_computation.4 | async-start | bytes 7077888 | tf_op jit(solution)/shard_map/all_gather | solution.py:82
  240.7 329.3 %all-reduce.106.cloned.1.call-start = ((), (), s32[]{:S(2)}) async-start(), calls=%async_computation.7 | async-start | bytes 18874368 | tf_op jit(solution)/shard_map/psum | solution.py:118
  328.2 10.6 %copy-start.50 = (bf16[1024,3072]{1,0:T(8,128)(2,1)S(1)}, bf16[1024,3072]{1,0:T(8,128)(2,1)}, u32[]{:S(2)}) copy-start(bf16[1024,3072]{1,0:T(8,128)(2,1)} %all-gather.5.cloned.1.call-done) | copy-start | bytes 18874372
  328.2 10.6 %copy-start.52 = (f32[768]{0:T(1024)S(1)}, f32[768]{0:T(1024)}, u32[]{:S(2)}) copy-start(f32[768]{0:T(1024)} %param.18) | copy-start | bytes 9220
  328.3 10.6 %copy-start.54 = (f32[1024,768]{1,0:T(8,128)S(1)}, f32[1024,768]{1,0:T(8,128)}, u32[]{:S(2)}) copy-start(f32[1024,768]{1,0:T(8,128)} %copy-done.53) | copy-start | bytes 9437188
  338.9 7.2 copy-start.55
  355.8 316.2 %reduce-scatter.5.cloned.1.call-start = ((), (), s32[]{:S(2)}) async-start(), calls=%async_computation.5 | async-start | bytes 7077888 | tf_op jit(solution)/shard_map/reduce_scatter | solution.py:95
  365.0 496.5 %all-reduce.104.cloned.1.call-start = ((), (), s32[]{:S(2)}) async-start(), calls=%async_computation.6 | async-start | bytes 1376256 | tf_op jit(solution)/shard_map/psum | solution.py:113
  570.0 5.6 copy-start.4
  686.1 3.4 copy-start.17
  686.1 3.4 copy-start.19
  686.1 3.4 copy-start.21
  686.1 3.4 copy-start.23
  686.1 3.4 copy-start.25
  686.2 3.4 copy-start.27
  686.2 3.4 copy-start.29
  686.2 3.4 copy-start.31
  686.2 3.4 copy-start.33
  689.7 6.1 copy-start.7
  689.7 6.1 copy-start.9
  689.7 6.1 copy-start.11
  689.7 6.1 copy-start.13
  689.7 6.1 copy-start.15
  716.7 28.4 %copy-start.42 = (f32[3072]{0:T(1024)S(1)}, f32[3072]{0:T(1024)}, u32[]{:S(2)}) copy-start(f32[3072]{0:T(1024)} %param.20) | copy-start | bytes 36868
  745.1 6.3 copy-start.43
  745.1 6.3 copy-start.44
  745.1 6.3 copy-start.45
  745.1 6.3 copy-start.46
  (14 other events, 31.6 us)
Sparse Core Ops, SparseCore 0:
  29.7 91.5 all-gather.2
  140.9 95.8 reduce-scatter.2
  240.8 87.3 all-gather.4
  355.9 214.0 all-reduce.105
  573.7 98.2 reduce-scatter.4
  716.8 144.6 all-reduce.103
where the time goes:
time: 871 us; the launch traced here: 870 us
  waiting for transfers between devices  585 us (67%)
  other arithmetic  111 us (13%)
  blocking collectives  95.5 us (11%)
  matrix products  54.4 us (6%)
  between operations  14.8 us (2%)
  local copies, waits for them, and re-layouts  9.77 us (1%)
    psum x1, waiting for transfers between devices, on_device(): lax.psum(part_up.astype(jnp.bfloat16), 'dp').astype(jnp.float32)  174 us
    reduce_scatter x1, waiting for transfers between devices, on_device(): lax.psum_scatter(jnp.dot(hidden, w_down, preferred_element_type=jnp.float...  96 us
    reduce_scatter x1, waiting for transfers between devices, on_device(): lax.psum_scatter(lax.dot_general(grad_pre, w_up, (((1,), (1,)), ((), ()))...  93.1 us
    all_gather x1, waiting for transfers between devices, on_device(): group_normed = lax.all_gather(normed, 'fsdp', axis=0, tiled=True)  91.7 us
    all_gather x1, waiting for transfers between devices, on_device(): group_scaled = lax.all_gather(scaled, 'fsdp', axis=0, tiled=True)  87.3 us
    psum x1, blocking collectives, on_device(): lax.psum((grad_kernel, grad_conv_bias, grad_gain, grad_shift, grad_down_b...  65.4 us
    psum x1, waiting for transfers between devices, on_device(): lax.psum((grad_kernel, grad_conv_bias, grad_gain, grad_shift, grad_down_b...  42.8 us
    psum x1, blocking collectives, on_device(): lax.psum(part_bias.astype(jnp.bfloat16), 'dp').astype(jnp.float32)  30.1 us
  transfers between devices with their start and end apart: 6, of which 6 were waited for; matrix products, arithmetic and copies ran while one was open for 6% of the time, Pallas kernels for 0%

commit v1 on v0

v1 whole, which is shorter than its diff:
```python
import math

import jax
import jax.numpy as jnp
from jax import lax
from jax.experimental import pallas as pl
from jax.experimental.pallas import tpu as pltpu
from jax.sharding import PartitionSpec as P

MESH = pl.DeviceIdType.MESH
F32 = jnp.float32
BF16 = jnp.bfloat16
CH = 3072
HID = 768
ROWS = 128
LANES = 128
BLOCKS = CH // LANES
ANY = pl.BlockSpec(memory_space=pl.ANY)
VMEM = pl.BlockSpec(memory_space=pltpu.VMEM)


class Place:
    def __init__(self):
        d = lax.axis_index("dp")
        f = lax.axis_index("fsdp")
        self.z = lax.div(d, 4)
        self.x_lo = lax.rem(lax.div(d, 2), 2)
        self.core = lax.rem(d, 2)
        self.y = lax.div(f, 2)
        self.x_hi = lax.rem(f, 2)
        self.x = self.x_hi * 2 + self.x_lo
        self.other_core = 1 - self.core
        self.x_cut = 3 - self.x
        self.x_pair = self.x_hi * 2 + (1 - self.x_lo)

    def at(self, x=None, y=None, z=None, core=None):
        x = self.x if x is None else x
        y = self.y if y is None else y
        z = self.z if z is None else z
        core = self.core if core is None else core
        return (z * 4 + lax.rem(x, 2) * 2 + core, y * 2 + lax.div(x, 2))

    def ring(self, axis):
        me = getattr(self, axis)
        right, left, far = lax.rem(me + 1, 4), lax.rem(me + 3, 4), lax.rem(me + 2, 4)
        return self.at(**{axis: right}), self.at(**{axis: left}), me, right, left, far


class Copies:
    def __init__(self, send, recv, local):
        self.send, self.recv, self.local = send, recv, local
        self.used = 0
        self.used_local = 0
        self.sent = []

    def remote(self, src, dst, device):
        index = self.used
        self.used += 1
        return pltpu.make_async_remote_copy(
            src_ref=src,
            dst_ref=dst,
            send_sem=self.send.at[index],
            recv_sem=self.recv.at[index],
            device_id=device,
            device_id_type=MESH,
        )

    def push(self, src, dst, device):
        copy = self.remote(src, dst, device)
        copy.start()
        self.sent.append(copy)
        return copy

    def here(self, src, dst):
        index = self.used_local
        self.used_local += 1
        copy = pltpu.make_async_copy(src, dst, self.local.at[index])
        copy.start()
        return copy

    def drain(self):
        for copy in self.sent:
            copy.wait_send()


def greet(devices):
    barrier = pltpu.get_barrier_semaphore()
    for device in devices:
        pl.semaphore_signal(barrier, inc=1, device_id=device, device_id_type=MESH)
    pl.semaphore_wait(barrier, len(devices))


def rows_at(start, size):
    return pl.ds(pl.multiple_of(start, 16), size)


def lanes_at(block):
    return pl.ds(pl.multiple_of(block * LANES, LANES), LANES)


def shifted(row, by):
    if by == 0:
        return row
    moved = pltpu.roll(row, (-by) % 8, 0)
    place = lax.broadcasted_iota(jnp.int32, row.shape, 0)
    inside = (place + by >= 0) & (place + by < 8)
    return jnp.where(inside, moved, 0.0)


def tile_rows(ref, block):
    tiles = []
    for pair in range(8):
        both = ref[16 * pair : 16 * pair + 16, lanes_at(block)].astype(F32)
        tiles += [both[:8], both[8:]]
    return tiles


def conv_block(block, img, dww, dwb, out):
    pixels = tile_rows(img, block)
    cs = lanes_at(block)
    sums = [jnp.broadcast_to(dwb[0:1, cs], (8, LANES))] * 16
    for horizontal in range(7):
        moved = [shifted(tile, horizontal - 3) for tile in pixels]
        for vertical in range(7):
            tap = vertical * 7 + horizontal
            weight = jnp.broadcast_to(dww[tap : tap + 1, cs], (8, LANES))
            for image in range(2):
                for p in range(8):
                    source = p + vertical - 3
                    if 0 <= source < 8:
                        sums[image * 8 + p] = sums[image * 8 + p] + moved[image * 8 + source] * weight
    for r in range(16):
        out[8 * r : 8 * r + 8, cs] = sums[r]


def first_kernel(
    img, gout, dww, dwb, gain, shift, lscale, wu, wd, bu,
    gn, gs, std, inv, wuo, wdo, buo,
    scaled, normed, bu_v, send, recv, local,
):
    me = Place()
    copies = Copies(send, recv, local)
    right, left, y, y_right, y_left, y_far = me.ring("y")
    cut = me.at(x=me.x_cut)
    pair = me.at(x=me.x_pair)
    mate = me.at(core=me.other_core)
    greet([right, left, cut, pair, mate])

    up_rows, down_rows, parts = 192, 48, 4
    theirs = (1 - me.x_lo) * 2 + me.core
    mine = me.x_lo * 2 + me.core
    pairs = (1 - me.x_lo) * 2 + me.core

    def chunk(matrix, quarter, part):
        size = up_rows if matrix == 0 else down_rows
        return rows_at(quarter * (size * parts) + part * size, size)

    order = [(m, k) for k in range(parts) for m in range(2)]
    over_cut = []
    bias = copies.push(bu, buo, cut)
    for m, k in order:
        src, dst = ((wu, wuo), (wd, wdo))[m]
        at = chunk(m, theirs, k)
        over_cut.append(copies.push(src.at[at], dst.at[at], cut))

    def scale_block(block, carry):
        cs = lanes_at(block)
        scaled[:, cs] = (gout[:, cs].astype(F32) * lscale[0:1, cs]).astype(BF16)
        return carry

    lax.fori_loop(0, BLOCKS, scale_block, 0)

    half = ROWS // 2
    low, high = pl.ds(0, half), pl.ds(half, half)

    def spread(src, dst):
        first = [copies.push(src.at[low], dst.at[y, low], right), copies.push(src.at[high], dst.at[y, high], left)]
        second = [copies.push(src.at[high], dst.at[y, high], right), copies.push(src.at[low], dst.at[y, low], left)]
        return first, second, copies.here(src, dst.at[y])

    def forward(first, dst):
        first[0].wait_recv()
        to_right = copies.push(dst.at[y_left, low], dst.at[y_left, low], right)
        first[1].wait_recv()
        to_left = copies.push(dst.at[y_right, high], dst.at[y_right, high], left)
        return [to_right, to_left]

    s_first, s_second, s_own = spread(scaled, gs)

    def conv_step(block, carry):
        conv_block(block, img, dww, dwb, std)
        return carry

    lax.fori_loop(0, BLOCKS, conv_step, 0)

    def add_block(block, total):
        return total + std[:, lanes_at(block)]

    zero = jnp.zeros((ROWS, LANES), F32)
    mean = jnp.sum(lax.fori_loop(0, BLOCKS, add_block, zero), axis=1, keepdims=True) * (1.0 / CH)

    def square_block(block, total):
        centred = std[:, lanes_at(block)] - mean
        return total + centred * centred

    variance = jnp.sum(lax.fori_loop(0, BLOCKS, square_block, zero), axis=1, keepdims=True) * (1.0 / CH)
    inv_std = lax.rsqrt(variance + 1e-06)
    inv[...] = jnp.broadcast_to(inv_std, (ROWS, LANES))

    def norm_block(block, carry):
        cs = lanes_at(block)
        standard = (std[:, cs] - mean) * inv_std
        std[:, cs] = standard
        normed[:, cs] = (standard * gain[0:1, cs] + shift[0:1, cs]).astype(BF16)
        return carry

    lax.fori_loop(0, BLOCKS, norm_block, 0)
    n_first, n_second, n_own = spread(normed, gn)
    s_last = forward(s_first, gs)

    def relay(index):
        m, k = order[index]
        dst = (wuo, wdo)[m]
        over_cut[index].wait_recv()
        at = chunk(m, mine, k)
        return copies.push(dst.at[at], dst.at[at], mate), copies.push(dst.at[at], dst.at[at], pair)

    def relay_pair(index, from_pair):
        m, k = order[index]
        dst = (wuo, wdo)[m]
        from_pair.wait_recv()
        at = chunk(m, pairs, k)
        return copies.push(dst.at[at], dst.at[at], mate)

    relayed, last = [], []
    for index in range(len(order)):
        relayed.append(relay(index))
        if index == 4:
            n_last = forward(n_first, gn)
        if index >= 1:
            last.append(relay_pair(index - 1, relayed[index - 1][1]))
    last.append(relay_pair(len(order) - 1, relayed[-1][1]))

    bias.wait_recv()
    for copy in s_second + n_second + s_last + n_last + [r[0] for r in relayed] + last:
        copy.wait_recv()
    s_own.wait()
    n_own.wait()
    copies.drain()


def first_call(img, gout, dww, dwb, gain, shift, lscale, wu, wd, bu):
    remote = 48
    return pl.pallas_call(
        first_kernel,
        out_shape=(
            jax.ShapeDtypeStruct((4, ROWS, CH), BF16),
            jax.ShapeDtypeStruct((4, ROWS, CH), BF16),
            jax.ShapeDtypeStruct((ROWS, CH), F32),
            jax.ShapeDtypeStruct((ROWS, LANES), F32),
            jax.ShapeDtypeStruct((CH, HID), BF16),
            jax.ShapeDtypeStruct((HID, CH), BF16),
            jax.ShapeDtypeStruct((8, LANES), F32),
        ),
        in_specs=[VMEM] * 7 + [ANY] * 3,
        out_specs=(ANY, ANY, VMEM, VMEM, ANY, ANY, ANY),
        scratch_shapes=[
            pltpu.VMEM((ROWS, CH), BF16),
            pltpu.VMEM((ROWS, CH), BF16),
            pltpu.VMEM((8, LANES), F32),
            pltpu.SemaphoreType.DMA((remote,)),
            pltpu.SemaphoreType.DMA((remote,)),
            pltpu.SemaphoreType.DMA((2,)),
        ],
        compiler_params=pltpu.CompilerParams(
            collective_id=0, has_side_effects=True, vmem_limit_bytes=40 * 1024 * 1024
        ),
    )(img, gout, dww, dwb, gain, shift, lscale, wu, wd, bu)


def add_rows(dst, dst_row, sources, rows, column, columns, step=16):
    def body(index, carry):
        at = rows_at(dst_row + index * step, step)
        cs = pl.ds(column, columns)
        total = dst[at, cs].astype(F32)
        for ref, row, first in sources:
            total = total + ref[rows_at(row + index * step, step), pl.ds(first, columns)].astype(F32)
        dst[at, cs] = total.astype(dst.dtype)
        return carry

    lax.fori_loop(0, rows // step, body, 0)


class RingSum:
    def __init__(self, copies, where, data, base, rows, near, far, step=16):
        self.copies, self.data, self.base, self.rows = copies, data, base, rows
        self.right, self.left, self.me, self.at_right, self.at_left, self.at_far = where
        self.near, self.far, self.step = near, far, step
        self.half = data.shape[1] // 2

    def block(self, which):
        return self.base + which * self.rows

    def begin(self):
        at = rows_at(self.block(self.at_far), self.rows) if self.step == 16 else pl.ds(self.block(self.at_far), self.rows)
        h = self.half
        self.one = [
            self.copies.push(self.data.at[at, pl.ds(0, h)], self.far.at[0], self.right),
            self.copies.push(self.data.at[at, pl.ds(h, h)], self.far.at[1], self.left),
        ]

    def middle(self):
        h = self.half
        self.two = []
        for side, (device, block) in enumerate(((self.right, self.at_right), (self.left, self.at_left))):
            self.one[side].wait_recv()
            start = self.block(block)
            add_rows(self.data, start, [(self.far.at[side], 0, 0)], self.rows, side * h, h, self.step)
            at = rows_at(start, self.rows)
            self.two.append(self.copies.push(self.data.at[at], self.near.at[side], device))

    def end(self):
        for copy in self.two:
            copy.wait_recv()
        add_rows(
            self.data,
            self.block(self.me),
            [(self.near.at[0], 0, 0), (self.near.at[1], 0, 0)],
            self.rows,
            0,
            2 * self.half,
            self.step,
        )


def small_add(dst, row, sources, rows):
    total = dst[row, :]
    for source in sources:
        total = total + source
    dst[row, :] = total


def second_kernel(
    pn, pb, gu, gd, img, gout, std, inv, dww, gain, lscale, bdown, pbias,
    out_img, grad_img, out_up, out_down, out_small,
    guv, gdv, cu, cd, d1a, d1b, u1a, u1b, d2a, d2b, u2a, u2b, tq, fd, fu,
    nv, bv, n1, n2, b1, b2, gcv, sm, smc, sya, syb, sx, sz, smo,
    send, recv, local,
):
    me = Place()
    copies = Copies(send, recv, local)
    ring_x, ring_y, ring_z = me.ring("x"), me.ring("y"), me.ring("z")
    mate = me.at(core=me.other_core)
    x_cut = me.at(x=me.x_cut)
    x_pair = me.at(x=me.x_pair)
    greet([ring_x[0], ring_x[1], ring_y[0], ring_y[1], ring_z[0], ring_z[1], mate])
    x, y, z = me.x, me.y, me.z
    factor = 1.0 / math.sqrt(16384.0)

    keep = lax.rem(me.x_hi + me.core, 2)
    give = 1 - keep
    z_far, z_right, z_left = ring_z[5], ring_z[3], ring_z[4]
    x_far, x_right, x_left = ring_x[5], ring_x[3], ring_x[4]
    order = [(0, z_far), (1, x_far), (0, z_right), (1, x_right), (0, z_left), (1, x_left), (0, z), (1, x)]
    swaps, loads = [], []

    def piece(matrix, which):
        return rows_at(which * 192, 192) if matrix == 0 else rows_at(which * 768, 768)

    for m, which in order:
        src, dst, mine = ((gd, cd, gdv), (gu, cu, guv))[m]
        at = piece(m, which)
        swaps.append(copies.push(src.at[give, at], dst.at[at], mate))
        loads.append(copies.here(src.at[keep, at], mine.at[at]))

    y_far = ring_y[5]
    load_n = copies.here(pn, nv)
    load_b = copies.here(pb, bv)
    load_n.wait()
    rs_n = RingSum(copies, ring_y, nv, 0, ROWS, n2, n1)
    rs_n.begin()
    load_b.wait()
    rs_b = RingSum(copies, ring_y, bv, 0, ROWS, b2, b1)

    def merge(index):
        m, which = order[index]
        mine, other = ((gdv, cd), (guv, cu))[m]
        rows = 192 if m == 0 else 768
        loads[index].wait()
        swaps[index].wait_recv()
        add_rows(mine, which * rows, [(other, which * rows, 0)], rows, 0, mine.shape[1], 16 if m == 0 else 64)

    rs_d1 = RingSum(copies, ring_z, gdv, 0, 192, d1b, d1a)
    rs_u1 = RingSum(copies, ring_x, guv, 0, 768, u1b, u1a)
    merge(0)
    rs_d1.begin()
    merge(1)
    rs_u1.begin()
    rs_b.begin()
    merge(2)
    merge(3)
    rs_n.middle()
    merge(4)
    merge(5)
    rs_d1.middle()
    rs_u1.middle()
    rs_b.middle()
    merge(6)
    merge(7)

    rs_n.end()
    own = y * ROWS
    zero = jnp.zeros((ROWS, LANES), F32)

    def own_rows(ref, cs):
        return ref[rows_at(own, ROWS), cs].astype(F32)

    def norm_sums(block, totals):
        cs = lanes_at(block)
        grad_normed = own_rows(nv, cs)
        standard = std[:, cs]
        product = grad_normed * standard
        sm[50:51, cs] = jnp.sum(product, axis=0, keepdims=True)
        sm[51:52, cs] = jnp.sum(grad_normed, axis=0, keepdims=True)
        weight = gain[0:1, cs]
        return totals[0] + grad_normed * weight, totals[1] + product * weight

    total_g, total_gs = lax.fori_loop(0, BLOCKS, norm_sums, (zero, zero))
    mean_g = jnp.sum(total_g, axis=1, keepdims=True) * (1.0 / CH)
    mean_gs = jnp.sum(total_gs, axis=1, keepdims=True) * (1.0 / CH)
    inv_std = inv[...]

    def norm_apply(block, carry):
        cs = lanes_at(block)
        grad_hat = own_rows(nv, cs) * gain[0:1, cs]
        grad_conv = inv_std * (grad_hat - mean_g - std[:, cs] * mean_gs)
        gcv[:, cs] = grad_conv
        sm[49:50, cs] = jnp.sum(grad_conv, axis=0, keepdims=True)
        upstream = gout[:, cs].astype(F32)
        scaled = (upstream * lscale[0:1, cs]).astype(BF16).astype(F32)
        sm[52:53, cs] = jnp.sum(scaled, axis=0, keepdims=True)
        return carry

    lax.fori_loop(0, BLOCKS, norm_apply, 0)

    rs_d1.end()
    rs_d2 = RingSum(copies, ring_x, gdv, z * 192, 48, d2b, d2a)
    rs_d2.begin()
    rs_u1.end()
    rs_u2 = RingSum(copies, ring_z, guv, x * 768, 192, u2b, u2a)
    rs_u2.begin()

    def conv_back(block, carry):
        cs = lanes_at(block)
        pixels = tile_rows(img, block)
        upstream = tile_rows(gout, block)
        grads = [gcv[8 * r : 8 * r + 8, cs] for r in range(16)]
        sums = upstream
        for horizontal in range(7):
            moved = [shifted(tile, 3 - horizontal) for tile in grads]
            for vertical in range(7):
                tap = vertical * 7 + horizontal
                weight = jnp.broadcast_to(dww[tap : tap + 1, cs], (8, LANES))
                taps = jnp.zeros((8, LANES), F32)
                for image in range(2):
                    for p in range(8):
                        source = p - (vertical - 3)
                        if 0 <= source < 8:
                            tile = moved[image * 8 + source]
                            sums[image * 8 + p] = sums[image * 8 + p] + tile * weight
                            taps = taps + tile * pixels[image * 8 + p]
                sm[tap : tap + 1, cs] = jnp.sum(taps, axis=0, keepdims=True)
        for r in range(8):
            grad_img[16 * r : 16 * r + 16, cs] = jnp.concatenate(sums[2 * r : 2 * r + 2], axis=0).astype(BF16)
        return carry

    lax.fori_loop(0, BLOCKS, conv_back, 0)

    rs_d2.middle()
    rs_u2.middle()

    rs_b.end()

    def result_block(block, carry):
        cs = lanes_at(block)
        branch = own_rows(bv, cs) + bdown[0:1, cs]
        upstream = gout[:, cs].astype(F32)
        sm[53:54, cs] = jnp.sum(upstream * branch, axis=0, keepdims=True)
        out_img[:, cs] = (img[:, cs].astype(F32) + lscale[0:1, cs] * branch).astype(BF16)
        return carry

    lax.fori_loop(0, BLOCKS, result_block, 0)

    sm[54:64, :] = jnp.zeros((10, CH), F32)
    for s in range(2):
        shard = y * 2 + (me.x_hi if s == 0 else 1 - me.x_hi)
        for line in range(2):

            @pl.when(lax.div(shard, 4) == line)
            def _(s=s, line=line):
                at = pl.ds(pl.multiple_of(lax.rem(shard, 4) * HID, LANES), HID)
                sm[54 + line : 55 + line, at] = pbias[s : s + 1, :]

    swap_small = copies.push(sm.at[pl.ds(pl.multiple_of(me.other_core * 32, 8), 32)], smc, mate)

    rs_d2.end()
    rs_u2.end()
    at_d = z * 192 + x * 48
    at_u = x * 768 + z * 192
    fd[...] = (gdv[rows_at(at_d, 48), :].astype(F32) * factor).astype(BF16)
    fu[...] = (guv[rows_at(at_u, 192), :].astype(F32) * factor).astype(BF16)
    needed = me.x_hi == me.core

    zr, zl = ring_z[0], ring_z[1]

    def slot(which):
        return rows_at(which * 192, 192)

    tq_own = copies.here(fu, tq.at[slot(z)])
    up_one = [copies.push(fu, tq.at[slot(z)], zr), copies.push(fu, tq.at[slot(z)], zl)]

    def drow(which_x, which_z=None):
        return rows_at((z if which_z is None else which_z) * 192 + which_x * 48, 48)

    d_cut = copies.remote(fd, out_down.at[drow(x)], x_cut)
    d_swap = copies.remote(fd, out_down.at[drow(x)], x_pair)
    d_cut_swap = copies.remote(out_down.at[drow(me.x_cut)], out_down.at[drow(me.x_cut)], x_pair)

    @pl.when(jnp.logical_not(needed))
    def _():
        d_cut.start()

    d_own = pltpu.make_async_copy(fd, out_down.at[drow(x)], local.at[20])

    @pl.when(needed)
    def _():
        d_own.start()
        d_swap.start()

    small_rows = me.core * 32
    swap_small.wait_recv()
    sm_at = pl.ds(pl.multiple_of(small_rows, 8), 32)
    sm[sm_at, :] = sm[sm_at, :] + smc[...]

    yr, yl, yy, y_right, y_left, y_far = ring_y

    def small_piece(which):
        return pl.ds(pl.multiple_of(small_rows + which * 8, 8), 8)

    h = CH // 2
    s_one = [
        copies.push(sm.at[small_piece(y_far), pl.ds(0, h)], sya.at[0], yr),
        copies.push(sm.at[small_piece(y_far), pl.ds(h, h)], sya.at[1], yl),
    ]

    up_one[0].wait_recv()
    z_left_slot, z_right_slot = slot(z_left), slot(z_right)
    hu = HID // 2
    up_two = [copies.push(tq.at[z_left_slot, pl.ds(0, hu)], tq.at[z_left_slot, pl.ds(0, hu)], zr)]
    up_one[1].wait_recv()
    up_two.append(copies.push(tq.at[z_right_slot, pl.ds(hu, hu)], tq.at[z_right_slot, pl.ds(hu, hu)], zl))

    s_two = []
    for side, (device, which) in enumerate(((yr, y_right), (yl, y_left))):
        s_one[side].wait_recv()
        at = small_piece(which)
        sm[at, pl.ds(side * h, h)] = sm[at, pl.ds(side * h, h)] + sya[side]
        s_two.append(copies.push(sm.at[at], syb.at[side], device))

    @pl.when(needed)
    def _():
        d_cut.wait_recv()
        d_cut_swap.start()

    for side in range(2):
        s_two[side].wait_recv()
    at = small_piece(yy)
    sx[pl.ds(x, 1)] = (sm[at, :] + syb[0] + syb[1])[None]

    def small_all(buffer, ring):
        to_right, to_left, where, _, at_left, _ = ring[0], ring[1], ring[2], ring[3], ring[4], ring[5]
        at_right = ring[3]
        one = [
            copies.push(buffer.at[where], buffer.at[where], to_right),
            copies.push(buffer.at[where], buffer.at[where], to_left),
        ]
        one[0].wait_recv()
        lo, hi = pl.ds(0, h), pl.ds(h, h)
        two = [copies.push(buffer.at[at_left, :, lo], buffer.at[at_left, :, lo], to_right)]
        one[1].wait_recv()
        two.append(copies.push(buffer.at[at_right, :, hi], buffer.at[at_right, :, hi], to_left))
        for copy in two:
            copy.wait_recv()
        return buffer[0] + buffer[1] + buffer[2] + buffer[3]

    sz[pl.ds(z, 1)] = small_all(sx, ring_x)[None]

    for copy in up_two:
        copy.wait_recv()
    tq_own.wait()

    def urow(which_x):
        return rows_at(which_x * 768, 768)

    u_cut = copies.remote(tq, out_up.at[urow(x)], x_cut)
    u_swap = copies.remote(tq, out_up.at[urow(x)], x_pair)
    u_mate = copies.remote(tq, out_up.at[urow(x)], mate)
    u_own = pltpu.make_async_copy(tq, out_up.at[urow(x)], local.at[21])

    @pl.when(jnp.logical_not(needed))
    def _():
        u_cut.start()

    @pl.when(needed)
    def _():
        u_swap.start()
        u_mate.start()
        u_own.start()

    total = small_all(sz, ring_z)
    smo_at = small_piece(yy)
    smo[smo_at, :] = total * factor

    def small_back():
        one = [
            copies.push(smo.at[smo_at], smo.at[smo_at], yr),
            copies.push(smo.at[smo_at], smo.at[smo_at], yl),
        ]
        lo, hi = pl.ds(0, h), pl.ds(h, h)
        from_left, from_right = small_piece(y_left), small_piece(y_right)
        one[0].wait_recv()
        two = [copies.push(smo.at[from_left, lo], smo.at[from_left, lo], yr)]
        one[1].wait_recv()
        two.append(copies.push(smo.at[from_right, hi], smo.at[from_right, hi], yl))
        for copy in two:
            copy.wait_recv()
        return copies.push(smo.at[sm_at], smo.at[sm_at], mate)

    small_mate = small_back()

    def dblock(which):
        return rows_at(which * 192, 192)

    hd = CH // 2
    lo, hi = pl.ds(0, hd), pl.ds(hd, hd)
    block, block_l, block_r, block_f = dblock(z), dblock(z_left), dblock(z_right), dblock(z_far)
    d_right = copies.remote(out_down.at[block], out_down.at[block], zr)
    d_left = copies.remote(out_down.at[block], out_down.at[block], zl)
    d_mate = copies.remote(out_down.at[block], out_down.at[block], mate)
    d_fwd_right = copies.remote(out_down.at[block_l, lo], out_down.at[block_l, lo], zr)
    d_fwd_left = copies.remote(out_down.at[block_r, hi], out_down.at[block_r, hi], zl)
    d_mate_l = copies.remote(out_down.at[block_l], out_down.at[block_l], mate)
    d_mate_r = copies.remote(out_down.at[block_r], out_down.at[block_r], mate)
    d_mate_f = copies.remote(out_down.at[block_f], out_down.at[block_f], mate)
    q_cut, q_pair, q_far = urow(me.x_cut), urow(me.x_pair), urow(3 - me.x_pair)
    u_cut_swap = copies.remote(out_up.at[q_cut], out_up.at[q_cut], x_pair)
    u_mate_c = copies.remote(out_up.at[q_cut], out_up.at[q_cut], mate)
    u_mate_p = copies.remote(out_up.at[q_pair], out_up.at[q_pair], mate)
    u_mate_f = copies.remote(out_up.at[q_far], out_up.at[q_far], mate)

    @pl.when(needed)
    def _():
        d_own.wait()
        d_swap.wait_recv()
        d_cut_swap.wait_recv()
        d_right.start()
        d_left.start()
        d_mate.start()
        u_cut.wait_recv()
        u_cut_swap.start()
        u_mate_c.start()
        d_right.wait_recv()
        d_fwd_right.start()
        d_mate_l.start()
        d_left.wait_recv()
        d_fwd_left.start()
        d_mate_r.start()
        u_swap.wait_recv()
        u_mate_p.start()
        d_fwd_right.wait_recv()
        d_fwd_left.wait_recv()
        d_mate_f.start()
        u_cut_swap.wait_recv()
        u_mate_f.start()
        u_own.wait()
        for copy in (
            d_swap, d_cut_swap, d_right, d_left, d_mate, d_fwd_right, d_fwd_left, d_mate_l, d_mate_r, d_mate_f,
            u_swap, u_mate, u_cut_swap, u_mate_c, u_mate_p, u_mate_f,
        ):
            copy.wait_send()

    @pl.when(jnp.logical_not(needed))
    def _():
        for copy in (d_mate, d_mate_l, d_mate_r, d_mate_f, u_mate, u_mate_c, u_mate_p, u_mate_f):
            copy.wait_recv()
        d_cut.wait_send()
        u_cut.wait_send()

    small_mate.wait_recv()
    out_small[...] = smo[...]
    copies.drain()


def second_call(*operands):
    remote = 80
    bf = lambda *shape: pltpu.VMEM(shape, BF16)
    fl = lambda *shape: pltpu.VMEM(shape, F32)
    return pl.pallas_call(
        second_kernel,
        out_shape=(
            jax.ShapeDtypeStruct((ROWS, CH), BF16),
            jax.ShapeDtypeStruct((ROWS, CH), BF16),
            jax.ShapeDtypeStruct((CH, HID), BF16),
            jax.ShapeDtypeStruct((HID, CH), BF16),
            jax.ShapeDtypeStruct((64, CH), F32),
        ),
        in_specs=[ANY] * 4 + [VMEM] * 9,
        out_specs=(VMEM, VMEM, ANY, ANY, VMEM),
        scratch_shapes=[
            bf(CH, HID), bf(HID, CH), bf(CH, HID), bf(HID, CH),
            bf(2, 192, 1536), bf(2, 192, 3072), bf(2, 768, 384), bf(2, 768, 768),
            bf(2, 48, 1536), bf(2, 48, 3072), bf(2, 192, 384), bf(2, 192, 768),
            bf(768, 768), bf(48, 3072), bf(192, 768),
            bf(512, CH), bf(512, CH),
            bf(2, 128, 1536), bf(2, 128, 3072), bf(2, 128, 1536), bf(2, 128, 3072),
            fl(ROWS, CH), fl(64, CH), fl(32, CH), fl(2, 8, 1536), fl(2, 8, CH),
            fl(4, 8, CH), fl(4, 8, CH), fl(64, CH),
            pltpu.SemaphoreType.DMA((remote,)),
            pltpu.SemaphoreType.DMA((remote,)),
            pltpu.SemaphoreType.DMA((24,)),
        ],
        compiler_params=pltpu.CompilerParams(
            collective_id=1, has_side_effects=True, vmem_limit_bytes=60 * 1024 * 1024
        ),
    )(*operands)


def gelu_exact(values):
    return 0.5 * values * (1.0 + lax.erf(values * 0.7071067811865476))


def gelu_slope(values):
    return (
        0.5 * (1.0 + lax.erf(values * 0.7071067811865476))
        + values * jnp.exp(-0.5 * values * values) * 0.3989422804014327
    )


def mlp(gn, gs, shards):
    nt = (((1,), (1,)), ((), ()))
    tn = (((0,), (0,)), ((), ()))
    branch = normed = 0.0
    ups, downs, biases = [], [], []
    for wu, wd, bu in shards:
        pre_up = jnp.dot(gn, wu, preferred_element_type=F32) + bu
        hidden = gelu_exact(pre_up).astype(BF16)
        grad_hidden = lax.dot_general(gs, wd, nt, preferred_element_type=F32)
        grad_pre = (grad_hidden * gelu_slope(pre_up)).astype(BF16)
        biases.append(jnp.sum(grad_pre, axis=0, dtype=F32))
        branch = branch + jnp.dot(hidden, wd, preferred_element_type=F32)
        normed = normed + lax.dot_general(grad_pre, wu, nt, preferred_element_type=F32)
        ups.append(lax.dot_general(gn, grad_pre, tn, preferred_element_type=F32).astype(BF16))
        downs.append(lax.dot_general(hidden, gs, tn, preferred_element_type=F32).astype(BF16))
    return normed.astype(BF16), branch.astype(BF16), jnp.stack(ups), jnp.stack(downs), jnp.stack(biases)


def on_device(
    images, grad_out, dw_weight, dw_bias, ln_gain, ln_bias, w_up, b_up, w_down, b_down, layer_scale
):
    img = images.reshape(ROWS, CH)
    gout = grad_out.reshape(ROWS, CH)
    dww = dw_weight.reshape(49, CH)
    row = lambda vector: vector.reshape(1, CH)
    bu = jnp.pad(b_up.reshape(6, LANES), ((0, 2), (0, 0)))
    gn, gs, std, inv, wuo, wdo, buo = first_call(
        img, gout, dww, row(dw_bias), row(ln_gain), row(ln_bias), row(layer_scale), w_up, w_down, bu
    )
    b_other = buo[:6].reshape(HID)
    pn, pb, gu, gd, pbias = mlp(
        gn.reshape(4 * ROWS, CH), gs.reshape(4 * ROWS, CH), ((w_up, w_down, b_up), (wuo, wdo, b_other))
    )
    out_img, grad_img, out_up, out_down, small = second_call(
        pn, pb, gu, gd, img, gout, std, inv, dww, row(ln_gain), row(layer_scale), row(b_down), pbias
    )
    shard = lax.axis_index("fsdp")
    grad_b_up = lax.dynamic_slice(small[54:56].reshape(-1), (shard * HID,), (HID,)).astype(BF16)
    return (
        out_img.reshape(images.shape),
        grad_img.reshape(images.shape),
        out_up,
        grad_b_up,
        out_down,
        small[:49].reshape(dw_weight.shape),
        small[49],
        small[50],
        small[51],
        small[52],
        small[53],
    )


def solution(mesh):
    tokens = P(("dp", "fsdp"), None, None, None)
    up, bias, down = P(None, "fsdp"), P("fsdp"), P("fsdp", None)
    return jax.shard_map(
        on_device,
        mesh=mesh,
        in_specs=(tokens, tokens, P(), P(), P(), P(), up, bias, down, P(), P()),
        out_specs=(tokens, tokens, up, bias, down, P(), P(), P(), P(), P(), P()),
        check_vma=False,
    )
```

time: 871 us -> 301 us (0.35)
  waiting for transfers between devices: 585 us -> 0 us
  Pallas kernels: 0 us -> 212 us
  blocking collectives: 95.5 us -> 0 us
  other arithmetic: 111 us -> 17.3 us
  between operations: 14.8 us -> 0.97 us
  local copies, waits for them, and re-layouts: 9.77 us -> 22.1 us
    psum x2 -> x0, waiting for transfers between devices: 216 us -> none  [the longest x1 174 us: on_device(): lax.psum(part_up.astype(jnp.bfloat16), 'dp').astype(jnp.float32)]
    pallas_call x0 -> x2, Pallas kernels: none -> 212 us  [the longest x1 142 us: second_call(): pl.pallas_call(second_kernel, out_shape=(jax.ShapeDtypeStruct((ROWS, CH),...]
    reduce_scatter x2 -> x0, waiting for transfers between devices: 189 us -> none  [the longest x1 96 us: on_device(): lax.psum_scatter(jnp.dot(hidden, w_down, preferred_element_type=jnp.float...]
    all_gather x2 -> x0, waiting for transfers between devices: 179 us -> none  [the longest x1 91.7 us: on_device(): group_normed = lax.all_gather(normed, 'fsdp', axis=0, tiled=True)]
    psum x2 -> x0, blocking collectives: 95.5 us -> none  [the longest x1 65.4 us: on_device(): lax.psum((grad_kernel, grad_conv_bias, grad_gain, grad_shift, grad_down_b...]
    reduce_sum x9 -> x0, other arithmetic: 39.6 us -> none  [the longest x1 13.7 us: layer_norm(): average = jnp.mean(before_norm, axis=-1, keepdims=True)]
    add_any x2 -> x0, other arithmetic: 30.1 us -> none  [the longest x1 28.3 us: depthwise(): padded[:, vertical:vertical + extent, horizontal:horizontal + extent, :]]
    mul x7 -> x0, other arithmetic: 29 us -> none  [the longest x3 25.2 us: depthwise(): padded[:, vertical:vertical + extent, horizontal:horizontal + extent, :]]
  transfers between devices with their start and end apart: 6 -> 0, of which waited for: 6 -> 0; matrix products, arithmetic and copies ran while one was open for 6% -> 0% of each run, Pallas kernels for 0% -> 0%
where the time goes in v1:
time: 301 us
  Pallas kernels  212 us (70%)
  matrix products  48.6 us (16%)
  local copies, waits for them, and re-layouts  22.1 us (7%)
  other arithmetic  17.3 us (6%)
    pallas_call x1, Pallas kernels, second_call(): pl.pallas_call(second_kernel, out_shape=(jax.ShapeDtypeStruct((ROWS, CH),...  142 us
    pallas_call x1, Pallas kernels, first_call(): pl.pallas_call(first_kernel, out_shape=(jax.ShapeDtypeStruct((4, ROWS, CH...  69.8 us
    unnamed x64, local copies, waits for them, and re-layouts  15.7 us
    dot_general x2, matrix products, mlp(): lax.dot_general(grad_pre, wu, nt, preferred_element_type=F32)  10.8 us
    dot_general x2, matrix products, mlp(): lax.dot_general(hidden, gs, tn, preferred_element_type=F32).astype(BF16)  10.2 us
    dot_general x2, matrix products, mlp(): lax.dot_general(gn, grad_pre, tn, preferred_element_type=F32).astype(BF16)  8.6 us
    another operation x1, other arithmetic, mlp(): jnp.stack(ups)  8.43 us
    another operation x1, other arithmetic, mlp(): jnp.stack(downs)  8.25 us

profile of v1, /device:TPU:1, one launch (start us, length us, event | category | flops | bytes accessed | tf_op | source)
XLA Modules:
  0.0 300.8 jit_solution(12511743434939750036)
XLA Ops:
  0.6 1.2 reshape.73.dww
  1.8 0.0 copy-start
  1.8 0.7 pad.4.bu
  2.6 1.1 copy-done.1
  3.7 1.1 copy-done.2
  4.8 0.7 copy-done.5
  5.5 0.7 copy-done.6
  6.2 0.7 copy-done.7
  7.0 0.7 copy-done.8
  7.7 69.8 %shard_map.194 = (bf16[4,128,3072]{2,1,0:T(8,128)(2,1)S(1)}, bf16[4,128,3072]{2,1,0:T(8,128)(2,1)S(1)}, f32[128,3072]{1,0:T(8,128)S(1)}, f32[128,128]{1,0:T(8,12...) custom-call(bf16[128,3072]{1,0:T(8,128)(2,1)S(1)} %bitcast.51, ...), custom_call_target="tpu_custom_call" | custom-call | tf_op jit(solution)/shard_map/pallas_call | solution.py:254
  77.5 0.0 slice-start.3
  77.5 0.0 slice-start.6
  77.5 2.6 convolution_add_fusion.1
  80.2 0.0 copy-done.3
  80.2 0.0 copy-done.4
  80.2 0.0 copy-start.15
  80.2 0.0 slice-done.2
  80.2 0.0 slice-done.3
  80.2 0.0 slice-start.7
  80.2 3.0 %convert_reduce_fusion.1 = (f32[768]{0:T(1024)S(1)}, bf16[512,768]{1,0:T(8,128)(2,1)S(1)}) fusion(f32[512,768]{1,0:T(8,128)S(1)} %convolution_add_fusion.1, bf16[512,3072]{1,0:T(8,128)(2,1)S(1)} %bitcast.60, bf16[768,3072]{1,0:T(8,128)(2,1)S(1)} %bitcast.71), kind=kOutput, calls=%fused_computation.27 | convolution fusion | flops 2420636928 | bytes 10226688 | tf_op jit(solution)/shard_map/dot_general | solution.py:757
  83.3 0.0 copy-start.18
  83.3 0.0 slice-start.4
  83.3 4.6 %fusion.18 = f32[512,3072]{1,0:T(8,128)} fusion(bf16[512,768]{1,0:T(8,128)(2,1)S(1)} %get-tuple-element.43, bf16[3072,768]{1,0:T(8,128)(2,1)S(1)} %copy-done.11), kind=kOutput, calls=%fused_computation.40 | convolution fusion | flops 2415919104 | bytes 11796480 | tf_op jit(solution)/shard_map/dot_general | solution.py:761
  87.9 0.0 slice-done.7
  87.9 0.0 slice-start.5
  87.9 2.6 convolution_add_fusion
  90.6 3.9 %convert_reduce_fusion = (f32[768]{0:T(1024)S(1)}, bf16[512,768]{1,0:T(8,128)(2,1)}) fusion(f32[512,768]{1,0:T(8,128)S(1)} %convolution_add_fusion, bf16[512,3072]{1,0:T(8,128)(2,1)S(1)} %bitcast.61, bf16[768,3072]{1,0:T(8,128)(2,1)S(1)} %bitcast.83), kind=kOutput, calls=%fused_computation.26 | convolution fusion | flops 2420636928 | bytes 10226688 | tf_op jit(solution)/shard_map/dot_general | solution.py:757
  94.5 6.2 %add_convert_fusion.1.pn = bf16[512,3072]{1,0:T(8,128)(2,1)} fusion(f32[512,3072]{1,0:T(8,128)} %fusion.18, bf16[512,768]{1,0:T(8,128)(2,1)} %get-tuple-element.41, bf16[3072,768]{1,0:T(8,128)(2,1)S(1)} %bitcast.85), kind=kOutput, calls=%fused_computation.3 | convolution fusion | flops 2419064832 | bytes 14942208 | tf_op jit(solution)/shard_map/dot_general | solution.py:761
  100.7 2.6 fusion.16
  103.3 0.0 copy-start.20
  103.4 4.2 %add_convert_fusion.pb = bf16[512,3072]{1,0:T(8,128)(2,1)} fusion(f32[512,3072]{1,0:T(8,128)S(1)} %fusion.16, bf16[768,3072]{1,0:T(8,128)(2,1)S(1)} %bitcast.83, f32[512,768]{1,0:T(8,128)S(1)} %convolution_add_fusion), kind=kOutput, calls=%fused_computation.2 | convolution fusion | flops 2421030912 | bytes 15728640 | tf_op jit(solution)/shard_map/dot_general | solution.py:760
  107.6 4.3 %fusion.1 = bf16[1,3072,768]{2,1,0:T(8,128)(2,1)} fusion(bf16[512,3072]{1,0:T(8,128)(2,1)S(1)} %bitcast.66, bf16[512,768]{1,0:T(8,128)(2,1)S(1)} %copy-done.20), kind=kOutput, calls=%fused_computation.9 | convolution fusion | flops 2418278400 | bytes 8650752 | tf_op jit(solution)/shard_map/dot_general | solution.py:762
  111.9 4.3 %fusion = bf16[1,3072,768]{2,1,0:T(8,128)(2,1)} fusion(bf16[512,3072]{1,0:T(8,128)(2,1)S(1)} %bitcast.67, bf16[512,768]{1,0:T(8,128)(2,1)S(1)} %copy-done.19), kind=kOutput, calls=%fused_computation.8 | convolution fusion | flops 2418278400 | bytes 8650752 | tf_op jit(solution)/shard_map/dot_general | solution.py:762
  116.2 8.4 %pad_maximum_fusion.gu = bf16[2,3072,768]{2,1,0:T(8,128)(2,1)} fusion(bf16[1,3072,768]{2,1,0:T(8,128)(2,1)} %fusion.1, bf16[1,3072,768]{2,1,0:T(8,128)(2,1)} %fusion), kind=kLoop, calls=%fused_computation | loop fusion | flops 4718592 | bytes 18874368 | tf_op jit(solution)/shard_map/stack | solution.py:764
  124.6 5.8 %fusion.3 = bf16[1,768,3072]{2,1,0:T(8,128)(2,1)} fusion(bf16[512,3072]{1,0:T(8,128)(2,1)S(1)} %bitcast.62, f32[512,768]{1,0:T(8,128)} %copy-done.17), kind=kOutput, calls=%fused_computation.11 | convolution fusion | flops 2420244480 | bytes 9437184 | tf_op jit(solution)/shard_map/dot_general | solution.py:763
  130.5 4.3 %fusion.2 = bf16[1,768,3072]{2,1,0:T(8,128)(2,1)} fusion(bf16[512,3072]{1,0:T(8,128)(2,1)S(1)} %bitcast.63, f32[512,768]{1,0:T(8,128)S(1)} %copy-done.16), kind=kOutput, calls=%fused_computation.10 | convolution fusion | flops 2420244480 | bytes 9437184 | tf_op jit(solution)/shard_map/dot_general | solution.py:763
  134.8 8.2 %pad_maximum_fusion.1.gd = bf16[2,768,3072]{2,1,0:T(8,128)(2,1)} fusion(bf16[1,768,3072]{2,1,0:T(8,128)(2,1)} %fusion.3, bf16[1,768,3072]{2,1,0:T(8,128)(2,1)} %fusion.2), kind=kLoop, calls=%fused_computation.1 | loop fusion | flops 4718592 | bytes 18874368 | tf_op jit(solution)/shard_map/stack | solution.py:764
  143.1 0.6 pad_maximum_fusion.2.pbias
  143.7 142.0 %shard_map.195 = (bf16[128,3072]{1,0:T(8,128)(2,1)}, bf16[128,3072]{1,0:T(8,128)(2,1)}, bf16[3072,768]{1,0:T(8,128)(2,1)}, bf16[768,3072]{1,0:T(8,128)(2,1)}, f32[64,3072]{1,0:T(8,128)}) custom-call(bf16[512,3072]{1,0:T(8,128)(2,1)} %add_convert_fusion.1.pn, bf16[512,3072]{1,0:T(8,128)(2,1)} %add_convert_fusion.pb, ...), custom_call_target="tpu_custom_call" | custom-call | tf_op jit(solution)/shard_map/pallas_call | solution.py:708
  285.7 1.0 slice_bitcast_fusion
  286.8 0.7 dynamic_slice.5
  287.4 1.1 slice.26
  288.6 0.9 reshape.85
  289.5 1.8 fusion.17
  291.3 0.9 copy.27
  292.2 0.9 copy.28
  293.1 5.5 %copy.29 = bf16[3072,768]{1,0:T(8,128)(2,1)} copy(bf16[3072,768]{1,0:T(8,128)(2,1)} %get-tuple-element.57) | data formatting | bytes 9437184
  298.6 2.2 copy.30
  (46 shorter events, 0.1 us)
Async XLA Ops:
  1.8 75.6 %copy-start = (f32[49,3072]{1,0:T(8,128)}, f32[49,3072]{1,0:T(8,128)S(1)}, u32[]{:S(2)}) copy-start(f32[49,3072]{1,0:T(8,128)S(1)} %reshape.73.dww) | copy-start | bytes 1806340
  2.6 1.1 copy-start.1
  3.7 1.1 copy-start.2
  4.8 0.7 copy-start.5
  5.5 0.7 copy-start.6
  6.2 0.7 copy-start.7
  7.0 0.7 copy-start.8
  7.7 69.8 %copy-start.11 = (bf16[3072,768]{1,0:T(8,128)(2,1)S(1)}, bf16[3072,768]{1,0:T(8,128)(2,1)}, u32[]{:S(2)}) copy-start(bf16[3072,768]{1,0:T(8,128)(2,1)} %wu.1) | copy-start | bytes 14155780
  7.7 69.8 %copy-start.14 = (f32[768]{0:T(1024)S(1)}, f32[768]{0:T(1024)}, u32[]{:S(2)}) copy-start(f32[768]{0:T(1024)} %param.18) | copy-start | bytes 9220
  7.7 72.5 %slice-start.2 = ((s8[4718592]{0:T(1024)(128)(4,1)}), s8[4194304]{0:T(1024)(128)(4,1)S(1)}, s32[]{:S(2)}) async-start(s8[4718592]{0:T(1024)(128)(4,1)} %bitcast.70), calls=%async_computation.2 | async-start | bytes 8388608
  77.5 2.7 copy-start.3
  77.5 2.7 copy-start.4
  77.5 13.1 %copy-start.9 = (bf16[4,128,3072]{2,1,0:T(8,128)(2,1)}, bf16[4,128,3072]{2,1,0:T(8,128)(2,1)S(1)}, u32[]{:S(2)}) copy-start(bf16[4,128,3072]{2,1,0:T(8,128)(2,1)S(1)} %get-tuple-element.23) | copy-start | bytes 9437188
  77.5 2.7 slice-start.3
  77.5 10.3 %slice-start.6 = ((s8[4718592]{0:T(1024)(128)(4,1)}), s8[524288]{0:T(1024)(128)(4,1)S(1)}, s32[]{:S(2)}) async-start(s8[4718592]{0:T(1024)(128)(4,1)} %bitcast.84), calls=%async_computation.6 | async-start | bytes 1048576
  80.2 20.5 %copy-start.15 = (f32[512,768]{1,0:T(8,128)}, f32[512,768]{1,0:T(8,128)S(1)}, u32[]{:S(2)}) copy-start(f32[512,768]{1,0:T(8,128)S(1)} %convolution_add_fusion.1) | copy-start | bytes 4718596
  80.2 7.7 %slice-start.7 = ((s8[4718592]{0:T(1024)(128)(4,1)}), s8[4194304]{0:T(1024)(128)(4,1)S(1)}, s32[]{:S(2)}) async-start(s8[4718592]{0:T(1024)(128)(4,1)} %bitcast.84), calls=%async_computation.7 | async-start | bytes 8388608
  83.3 4.6 %copy-start.18 = (bf16[512,768]{1,0:T(8,128)(2,1)}, bf16[512,768]{1,0:T(8,128)(2,1)S(1)}, u32[]{:S(2)}) copy-start(bf16[512,768]{1,0:T(8,128)(2,1)S(1)} %get-tuple-element.43) | copy-start | bytes 2359300
  83.3 7.3 %slice-start.4 = ((s8[4718592]{0:T(1024)(128)(4,1)}), s8[524288]{0:T(1024)(128)(4,1)S(1)}, s32[]{:S(2)}) async-start(s8[4718592]{0:T(1024)(128)(4,1)} %bitcast.82), calls=%async_computation.4 | async-start | bytes 1048576
  87.9 2.7 slice-start.5
  90.5 12.8 %copy-start.17 = (f32[512,768]{1,0:T(8,128)}, f32[512,768]{1,0:T(8,128)S(1)}, u32[]{:S(2)}) copy-start(f32[512,768]{1,0:T(8,128)S(1)} %convolution_add_fusion) | copy-start | bytes 4718596
  103.3 4.2 %copy-start.20 = (bf16[512,768]{1,0:T(8,128)(2,1)S(1)}, bf16[512,768]{1,0:T(8,128)(2,1)}, u32[]{:S(2)}) copy-start(bf16[512,768]{1,0:T(8,128)(2,1)} %get-tuple-element.41) | copy-start | bytes 2359300
  107.6 4.3 %copy-start.19 = (bf16[512,768]{1,0:T(8,128)(2,1)S(1)}, bf16[512,768]{1,0:T(8,128)(2,1)}, u32[]{:S(2)}) copy-start(bf16[512,768]{1,0:T(8,128)(2,1)} %copy-done.18) | copy-start | bytes 2359300
  116.2 8.4 %copy-start.10 = (bf16[4,128,3072]{2,1,0:T(8,128)(2,1)S(1)}, bf16[4,128,3072]{2,1,0:T(8,128)(2,1)}, u32[]{:S(2)}) copy-start(bf16[4,128,3072]{2,1,0:T(8,128)(2,1)} %copy-done.9) | copy-start | bytes 9437188
  124.6 5.8 %copy-start.16 = (f32[512,768]{1,0:T(8,128)S(1)}, f32[512,768]{1,0:T(8,128)}, u32[]{:S(2)}) copy-start(f32[512,768]{1,0:T(8,128)} %copy-done.15) | copy-start | bytes 4718596
  285.7 5.6 %copy-start.13 = (bf16[128,3072]{1,0:T(8,128)(2,1)S(1)}, bf16[128,3072]{1,0:T(8,128)(2,1)}, u32[]{:S(2)}) copy-start(bf16[128,3072]{1,0:T(8,128)(2,1)} %get-tuple-element.30) | copy-start | bytes 2359300
  285.7 6.5 %copy-start.12 = (bf16[128,3072]{1,0:T(8,128)(2,1)S(1)}, bf16[128,3072]{1,0:T(8,128)(2,1)}, u32[]{:S(2)}) copy-start(bf16[128,3072]{1,0:T(8,128)(2,1)} %get-tuple-element.31) | copy-start | bytes 2359300
  292.2 6.4 %slice-start = ((s8[4718592]{0:T(1024)(128)(4,1)}), s8[4194304]{0:T(1024)(128)(4,1)S(1)}, s32[]{:S(2)}) async-start(s8[4718592]{0:T(1024)(128)(4,1)} %bitcast.68), calls=%async_computation | async-start | bytes 8388608
  293.1 5.5 %slice-start.1 = ((s8[4718592]{0:T(1024)(128)(4,1)}), s8[524288]{0:T(1024)(128)(4,1)S(1)}, s32[]{:S(2)}) async-start(s8[4718592]{0:T(1024)(128)(4,1)} %bitcast.68), calls=%async_computation.1 | async-start | bytes 1048576

commit v2 on v1

--- a/solution.py
+++ b/solution.py
@@ -133,10 +133,20 @@
         out[8 * r : 8 * r + 8, cs] = sums[r]
 
 
+def gelu_parts(values):
+    cdf = 0.5 * (1.0 + lax.erf(values * 0.7071067811865476))
+    return values * cdf, cdf + values * jnp.exp(-0.5 * values * values) * 0.3989422804014327
+
+
+NT = (((1,), (1,)), ((), ()))
+TN = (((0,), (0,)), ((), ()))
+
+
 def first_kernel(
     img, gout, dww, dwb, gain, shift, lscale, wu, wd, bu,
-    gn, gs, std, inv, wuo, wdo, buo,
-    scaled, normed, bu_v, send, recv, local,
+    std, inv, pn, pb, keep_up, keep_down, got_up, got_down, bias_sums,
+    gn, gs, wuv, wdv, bo, hid, gp, keep32, pnv, pbv, up_v, down_v,
+    send, recv, local,
 ):
     me = Place()
     copies = Copies(send, recv, local)
@@ -144,54 +154,85 @@
     cut = me.at(x=me.x_cut)
     pair = me.at(x=me.x_pair)
     mate = me.at(core=me.other_core)
+    wu_load = copies.here(wu, wuv.at[0])
+    wd_load = copies.here(wd, wdv.at[0])
     greet([right, left, cut, pair, mate])
 
     up_rows, down_rows, parts = 192, 48, 4
     theirs = (1 - me.x_lo) * 2 + me.core
     mine = me.x_lo * 2 + me.core
     pairs = (1 - me.x_lo) * 2 + me.core
+    weights = (wuv.at[1], wdv.at[1])
 
     def chunk(matrix, quarter, part):
         size = up_rows if matrix == 0 else down_rows
         return rows_at(quarter * (size * parts) + part * size, size)
 
-    order = [(m, k) for k in range(parts) for m in range(2)]
+    order = [(m, k) for m in range(2) for k in range(parts)]
+    bias = copies.push(bu, bo, cut)
     over_cut = []
-    bias = copies.push(bu, buo, cut)
     for m, k in order:
-        src, dst = ((wu, wuo), (wd, wdo))[m]
         at = chunk(m, theirs, k)
-        over_cut.append(copies.push(src.at[at], dst.at[at], cut))
+        over_cut.append(copies.push((wu, wd)[m].at[at], weights[m].at[at], cut))
+
+    own = rows_at(y * ROWS, ROWS)
 
     def scale_block(block, carry):
         cs = lanes_at(block)
-        scaled[:, cs] = (gout[:, cs].astype(F32) * lscale[0:1, cs]).astype(BF16)
+        gs[own, cs] = (gout[:, cs].astype(F32) * lscale[0:1, cs]).astype(BF16)
         return carry
 
     lax.fori_loop(0, BLOCKS, scale_block, 0)
 
     half = ROWS // 2
-    low, high = pl.ds(0, half), pl.ds(half, half)
-
-    def spread(src, dst):
-        first = [copies.push(src.at[low], dst.at[y, low], right), copies.push(src.at[high], dst.at[y, high], left)]
-        second = [copies.push(src.at[high], dst.at[y, high], right), copies.push(src.at[low], dst.at[y, low], left)]
-        return first, second, copies.here(src, dst.at[y])
-
-    def forward(first, dst):
+
+    def halves(position):
+        return rows_at(position * ROWS, half), rows_at(position * ROWS + half, half)
+
+    def spread(buffer):
+        low, high = halves(y)
+        first = [copies.push(buffer.at[low], buffer.at[low], right), copies.push(buffer.at[high], buffer.at[high], left)]
+        second = [copies.push(buffer.at[high], buffer.at[high], right), copies.push(buffer.at[low], buffer.at[low], left)]
+        return first, second
+
+    def forward(first, buffer):
+        low, high = halves(y_left)[0], halves(y_right)[1]
         first[0].wait_recv()
-        to_right = copies.push(dst.at[y_left, low], dst.at[y_left, low], right)
+        to_right = copies.push(buffer.at[low], buffer.at[low], right)
         first[1].wait_recv()
-        to_left = copies.push(dst.at[y_right, high], dst.at[y_right, high], left)
+        to_left = copies.push(buffer.at[high], buffer.at[high], left)
         return [to_right, to_left]
 
-    s_first, s_second, s_own = spread(scaled, gs)
+    relayed, last = {}, {}
+
+    def relay(index):
+        m, k = order[index]
+        over_cut[index].wait_recv()
+        at = chunk(m, mine, k)
+        ref = weights[m].at[at]
+        relayed[index] = copies.push(ref, ref, pair), copies.push(ref, ref, mate)
+
+    def relay_pair(index):
+        m, k = order[index]
+        relayed[index][0].wait_recv()
+        at = chunk(m, pairs, k)
+        ref = weights[m].at[at]
+        last[index] = copies.push(ref, ref, mate)
+
+    def arrived(indices):
+        for index in indices:
+            relayed[index][1].wait_recv()
+            last[index].wait_recv()
+
+    s_first, s_second = spread(gs)
 
     def conv_step(block, carry):
         conv_block(block, img, dww, dwb, std)
         return carry
 
-    lax.fori_loop(0, BLOCKS, conv_step, 0)
+    lax.fori_loop(0, BLOCKS // 2, conv_step, 0)
+    relay(0)
+    lax.fori_loop(BLOCKS // 2, BLOCKS, conv_step, 0)
 
     def add_block(block, total):
         return total + std[:, lanes_at(block)]
@@ -211,69 +252,216 @@
         cs = lanes_at(block)
         standard = (std[:, cs] - mean) * inv_std
         std[:, cs] = standard
-        normed[:, cs] = (standard * gain[0:1, cs] + shift[0:1, cs]).astype(BF16)
+        gn[own, cs] = (standard * gain[0:1, cs] + shift[0:1, cs]).astype(BF16)
         return carry
 
     lax.fori_loop(0, BLOCKS, norm_block, 0)
-    n_first, n_second, n_own = spread(normed, gn)
+    n_first, n_second = spread(gn)
+    relay(1)
     s_last = forward(s_first, gs)
 
-    def relay(index):
-        m, k = order[index]
-        dst = (wuo, wdo)[m]
-        over_cut[index].wait_recv()
-        at = chunk(m, mine, k)
-        return copies.push(dst.at[at], dst.at[at], mate), copies.push(dst.at[at], dst.at[at], pair)
-
-    def relay_pair(index, from_pair):
-        m, k = order[index]
-        dst = (wuo, wdo)[m]
-        from_pair.wait_recv()
-        at = chunk(m, pairs, k)
-        return copies.push(dst.at[at], dst.at[at], mate)
-
-    relayed, last = [], []
-    for index in range(len(order)):
-        relayed.append(relay(index))
-        if index == 4:
-            n_last = forward(n_first, gn)
-        if index >= 1:
-            last.append(relay_pair(index - 1, relayed[index - 1][1]))
-    last.append(relay_pair(len(order) - 1, relayed[-1][1]))
-
+    tile = 256
+
+    def hidden_tile(index):
+        return pl.ds(pl.multiple_of(index * tile, tile), tile)
+
+    bias_sums[...] = jnp.zeros_like(bias_sums)
+
+    def up_rows_of(s, position):
+        at = rows_at(position * ROWS, ROWS)
+
+        def body(index, carry):
+            cs = hidden_tile(index)
+            pre = jnp.dot(gn[at, :], wuv[s, :, cs], preferred_element_type=F32)
+            value, slope = gelu_parts(pre + (bu if s == 0 else bo)[0:1, cs])
+            hid[s, at, cs] = value.astype(BF16)
+            keep32[s, at, cs] = slope
+            return carry
+
+        lax.fori_loop(0, HID // tile, body, 0)
+
+    def grad_of(s):
+        def body(index, carry):
+            cs = hidden_tile(index)
+            grad = lax.dot_general(gs[...], wdv[s, cs, :], NT, preferred_element_type=F32)
+            pre = (grad * keep32[s, :, cs]).astype(BF16)
+            gp[s, :, cs] = pre
+            bias_sums[s : s + 1, cs] = jnp.sum(pre.astype(F32), axis=0, keepdims=True)
+            return carry
+
+        lax.fori_loop(0, HID // tile, body, 0)
+
+    keep = lax.rem(me.x_hi + me.core, 2)
+    moves = {}
+
+    def place(matrix, s, part):
+        if matrix == 0:
+            at = (pl.ds(part * 768, 768), slice(None))
+            mine, there, ref = keep_up, got_up, up_v
+        else:
+            at = (slice(None), pl.ds(part * 768, 768))
+            mine, there, ref = keep_down, got_down, down_v
+        if (matrix, part) not in moves:
+            index = copies.used_local
+            copies.used_local += 1
+            moves[matrix, part] = (
+                copies.remote(ref.at[at], there.at[at], mate),
+                pltpu.make_async_copy(ref.at[at], mine.at[at], local.at[index]),
+            )
+        away, stay = moves[matrix, part]
+
+        @pl.when(keep != s)
+        def _():
+            away.start()
+
+        @pl.when(keep == s)
+        def _():
+            stay.start()
+
+    def placed(matrix, s, part):
+        away, stay = moves[matrix, part]
+
+        @pl.when(keep != s)
+        def _():
+            away.wait_send()
+
+        @pl.when(keep == s)
+        def _():
+            stay.wait()
+
+    def part_up(s):
+        for part in range(4):
+            if s == 1:
+                placed(0, 0, part)
+
+            def body(index, carry, part=part):
+                rows = pl.ds(pl.multiple_of(part * 768 + index * tile, tile), tile)
+                up_v[rows, :] = lax.dot_general(gn[:, rows], gp[s], TN, preferred_element_type=F32).astype(BF16)
+                return carry
+
+            lax.fori_loop(0, 768 // tile, body, 0)
+            place(0, s, part)
+
+    def part_down(s):
+        for part in range(4):
+            if s == 1:
+                placed(1, 0, part)
+
+            def body(index, carry, part=part):
+                cs = pl.ds(pl.multiple_of(part * 768 + index * tile, tile), tile)
+                down_v[:, cs] = lax.dot_general(hid[s], gs[:, cs], TN, preferred_element_type=F32).astype(BF16)
+                return carry
+
+            lax.fori_loop(0, 768 // tile, body, 0)
+            place(1, s, part)
+
+    wu_load.wait()
+    relay(2)
+    relay_pair(0)
+    up_rows_of(0, y)
+    relay_pair(1)
+    relay(3)
+    relay_pair(2)
+    n_last = forward(n_first, gn)
+    relay(4)
+    relay_pair(3)
+    for copy in n_second:
+        copy.wait_recv()
+    up_rows_of(0, y_right)
+    up_rows_of(0, y_left)
+    relay(5)
+    relay_pair(4)
     bias.wait_recv()
-    for copy in s_second + n_second + s_last + n_last + [r[0] for r in relayed] + last:
+    arrived(range(4))
+    up_rows_of(1, y)
+    up_rows_of(1, y_right)
+    relay(6)
+    relay_pair(5)
+    up_rows_of(1, y_left)
+    wd_load.wait()
+    for copy in s_second + s_last:
         copy.wait_recv()
-    s_own.wait()
-    n_own.wait()
+    relay(7)
+    relay_pair(6)
+    for copy in n_last:
+        copy.wait_recv()
+    up_rows_of(0, y_far)
+    relay_pair(7)
+    grad_of(0)
+    up_rows_of(1, y_far)
+    part_up(0)
+    part_down(0)
+    arrived(range(4, 8))
+    grad_of(1)
+    part_up(1)
+    part_down(1)
+
+    def normed_back(index, carry):
+        cs = pl.ds(pl.multiple_of(index * tile, tile), tile)
+        total = lax.dot_general(gp[0], wuv[0, cs, :], NT, preferred_element_type=F32)
+        total = total + lax.dot_general(gp[1], wuv[1, cs, :], NT, preferred_element_type=F32)
+        pnv[:, cs] = total.astype(BF16)
+        return carry
+
+    lax.fori_loop(0, CH // tile, normed_back, 0)
+    pn_out = copies.here(pnv, pn)
+
+    def branch_tile(index, carry):
+        cs = pl.ds(pl.multiple_of(index * tile, tile), tile)
+        total = jnp.dot(hid[0], wdv[0, :, cs], preferred_element_type=F32)
+        total = total + jnp.dot(hid[1], wdv[1, :, cs], preferred_element_type=F32)
+        pbv[:, cs] = total.astype(BF16)
+        return carry
+
+    lax.fori_loop(0, CH // tile, branch_tile, 0)
+    pb_out = copies.here(pbv, pb)
+
+    pn_out.wait()
+    pb_out.wait()
+    for matrix in range(2):
+        for part in range(4):
+            placed(matrix, 1, part)
+            moves[matrix, part][0].wait_recv()
     copies.drain()
 
 
 def first_call(img, gout, dww, dwb, gain, shift, lscale, wu, wd, bu):
-    remote = 48
+    remote = 56
+    rows = 4 * ROWS
     return pl.pallas_call(
         first_kernel,
         out_shape=(
-            jax.ShapeDtypeStruct((4, ROWS, CH), BF16),
-            jax.ShapeDtypeStruct((4, ROWS, CH), BF16),
             jax.ShapeDtypeStruct((ROWS, CH), F32),
             jax.ShapeDtypeStruct((ROWS, LANES), F32),
+            jax.ShapeDtypeStruct((rows, CH), BF16),
+            jax.ShapeDtypeStruct((rows, CH), BF16),
             jax.ShapeDtypeStruct((CH, HID), BF16),
             jax.ShapeDtypeStruct((HID, CH), BF16),
-            jax.ShapeDtypeStruct((8, LANES), F32),
+            jax.ShapeDtypeStruct((CH, HID), BF16),
+            jax.ShapeDtypeStruct((HID, CH), BF16),
+            jax.ShapeDtypeStruct((8, HID), F32),
         ),
-        in_specs=[VMEM] * 7 + [ANY] * 3,
-        out_specs=(ANY, ANY, VMEM, VMEM, ANY, ANY, ANY),
+        in_specs=[VMEM] * 7 + [ANY, ANY, VMEM],
+        out_specs=(VMEM, VMEM, ANY, ANY, ANY, ANY, ANY, ANY, VMEM),
         scratch_shapes=[
-            pltpu.VMEM((ROWS, CH), BF16),
-            pltpu.VMEM((ROWS, CH), BF16),
-            pltpu.VMEM((8, LANES), F32),
+            pltpu.VMEM((rows, CH), BF16),
+            pltpu.VMEM((rows, CH), BF16),
+            pltpu.VMEM((2, CH, HID), BF16),
+            pltpu.VMEM((2, HID, CH), BF16),
+            pltpu.VMEM((8, HID), F32),
+            pltpu.VMEM((2, rows, HID), BF16),
+            pltpu.VMEM((2, rows, HID), BF16),
+            pltpu.VMEM((2, rows, HID), F32),
+            pltpu.VMEM((rows, CH), BF16),
+            pltpu.VMEM((rows, CH), BF16),
+            pltpu.VMEM((CH, HID), BF16),
+            pltpu.VMEM((HID, CH), BF16),
             pltpu.SemaphoreType.DMA((remote,)),
             pltpu.SemaphoreType.DMA((remote,)),
-            pltpu.SemaphoreType.DMA((2,)),
+            pltpu.SemaphoreType.DMA((12,)),
         ],
         compiler_params=pltpu.CompilerParams(
-            collective_id=0, has_side_effects=True, vmem_limit_bytes=40 * 1024 * 1024
+            collective_id=0, has_side_effects=True, vmem_limit_bytes=62 * 1024 * 1024
         ),
     )(img, gout, dww, dwb, gain, shift, lscale, wu, wd, bu)
 
@@ -341,7 +529,7 @@
 
 
 def second_kernel(
-    pn, pb, gu, gd, img, gout, std, inv, dww, gain, lscale, bdown, pbias,
+    pn, pb, gu, gd, ru, rd, img, gout, std, inv, dww, gain, lscale, bdown, pbias,
     out_img, grad_img, out_up, out_down, out_small,
     guv, gdv, cu, cd, d1a, d1b, u1a, u1b, d2a, d2b, u2a, u2b, tq, fd, fu,
     nv, bv, n1, n2, b1, b2, gcv, sm, smc, sya, syb, sx, sz, smo,
@@ -357,8 +545,6 @@
     x, y, z = me.x, me.y, me.z
     factor = 1.0 / math.sqrt(16384.0)
 
-    keep = lax.rem(me.x_hi + me.core, 2)
-    give = 1 - keep
     z_far, z_right, z_left = ring_z[5], ring_z[3], ring_z[4]
     x_far, x_right, x_left = ring_x[5], ring_x[3], ring_x[4]
     order = [(0, z_far), (1, x_far), (0, z_right), (1, x_right), (0, z_left), (1, x_left), (0, z), (1, x)]
@@ -368,10 +554,10 @@
         return rows_at(which * 192, 192) if matrix == 0 else rows_at(which * 768, 768)
 
     for m, which in order:
-        src, dst, mine = ((gd, cd, gdv), (gu, cu, guv))[m]
+        src, got, dst, mine = ((gd, rd, cd, gdv), (gu, ru, cu, guv))[m]
         at = piece(m, which)
-        swaps.append(copies.push(src.at[give, at], dst.at[at], mate))
-        loads.append(copies.here(src.at[keep, at], mine.at[at]))
+        swaps.append(copies.here(got.at[at], dst.at[at]))
+        loads.append(copies.here(src.at[at], mine.at[at]))
 
     y_far = ring_y[5]
     load_n = copies.here(pn, nv)
@@ -387,7 +573,7 @@
         mine, other = ((gdv, cd), (guv, cu))[m]
         rows = 192 if m == 0 else 768
         loads[index].wait()
-        swaps[index].wait_recv()
+        swaps[index].wait()
         add_rows(mine, which * rows, [(other, which * rows, 0)], rows, 0, mine.shape[1], 16 if m == 0 else 64)
 
     rs_d1 = RingSum(copies, ring_z, gdv, 0, 192, d1b, d1a)
@@ -530,7 +716,7 @@
     def _():
         d_cut.start()
 
-    d_own = pltpu.make_async_copy(fd, out_down.at[drow(x)], local.at[20])
+    d_own = pltpu.make_async_copy(fd, out_down.at[drow(x)], local.at[30])
 
     @pl.when(needed)
     def _():
@@ -605,7 +791,7 @@
     u_cut = copies.remote(tq, out_up.at[urow(x)], x_cut)
     u_swap = copies.remote(tq, out_up.at[urow(x)], x_pair)
     u_mate = copies.remote(tq, out_up.at[urow(x)], mate)
-    u_own = pltpu.make_async_copy(tq, out_up.at[urow(x)], local.at[21])
+    u_own = pltpu.make_async_copy(tq, out_up.at[urow(x)], local.at[31])
 
     @pl.when(jnp.logical_not(needed))
     def _():
@@ -714,7 +900,7 @@
             jax.ShapeDtypeStruct((HID, CH), BF16),
             jax.ShapeDtypeStruct((64, CH), F32),
         ),
-        in_specs=[ANY] * 4 + [VMEM] * 9,
+        in_specs=[ANY] * 6 + [VMEM] * 9,
         out_specs=(VMEM, VMEM, ANY, ANY, VMEM),
         scratch_shapes=[
             bf(CH, HID), bf(HID, CH), bf(CH, HID), bf(HID, CH),
@@ -727,41 +913,12 @@
             fl(4, 8, CH), fl(4, 8, CH), fl(64, CH),
             pltpu.SemaphoreType.DMA((remote,)),
             pltpu.SemaphoreType.DMA((remote,)),
-            pltpu.SemaphoreType.DMA((24,)),
+            pltpu.SemaphoreType.DMA((32,)),
         ],
         compiler_params=pltpu.CompilerParams(
             collective_id=1, has_side_effects=True, vmem_limit_bytes=60 * 1024 * 1024
         ),
     )(*operands)
-
-
-def gelu_exact(values):
-    return 0.5 * values * (1.0 + lax.erf(values * 0.7071067811865476))
-
-
-def gelu_slope(values):
-    return (
-        0.5 * (1.0 + lax.erf(values * 0.7071067811865476))
-        + values * jnp.exp(-0.5 * values * values) * 0.3989422804014327
-    )
-
-
-def mlp(gn, gs, shards):
-    nt = (((1,), (1,)), ((), ()))
-    tn = (((0,), (0,)), ((), ()))
-    branch = normed = 0.0
-    ups, downs, biases = [], [], []
-    for wu, wd, bu in shards:
-        pre_up = jnp.dot(gn, wu, preferred_element_type=F32) + bu
-        hidden = gelu_exact(pre_up).astype(BF16)
-        grad_hidden = lax.dot_general(gs, wd, nt, preferred_element_type=F32)
-        grad_pre = (grad_hidden * gelu_slope(pre_up)).astype(BF16)
-        biases.append(jnp.sum(grad_pre, axis=0, dtype=F32))
-        branch = branch + jnp.dot(hidden, wd, preferred_element_type=F32)
-        normed = normed + lax.dot_general(grad_pre, wu, nt, preferred_element_type=F32)
-        ups.append(lax.dot_general(gn, grad_pre, tn, preferred_element_type=F32).astype(BF16))
-        downs.append(lax.dot_general(hidden, gs, tn, preferred_element_type=F32).astype(BF16))
-    return normed.astype(BF16), branch.astype(BF16), jnp.stack(ups), jnp.stack(downs), jnp.stack(biases)
 
 
 def on_device(
@@ -771,16 +928,12 @@
     gout = grad_out.reshape(ROWS, CH)
     dww = dw_weight.reshape(49, CH)
     row = lambda vector: vector.reshape(1, CH)
-    bu = jnp.pad(b_up.reshape(6, LANES), ((0, 2), (0, 0)))
-    gn, gs, std, inv, wuo, wdo, buo = first_call(
+    bu = jnp.broadcast_to(b_up.reshape(1, HID), (8, HID))
+    std, inv, pn, pb, keep_up, keep_down, got_up, got_down, pbias = first_call(
         img, gout, dww, row(dw_bias), row(ln_gain), row(ln_bias), row(layer_scale), w_up, w_down, bu
     )
-    b_other = buo[:6].reshape(HID)
-    pn, pb, gu, gd, pbias = mlp(
-        gn.reshape(4 * ROWS, CH), gs.reshape(4 * ROWS, CH), ((w_up, w_down, b_up), (wuo, wdo, b_other))
-    )
     out_img, grad_img, out_up, out_down, small = second_call(
-        pn, pb, gu, gd, img, gout, std, inv, dww, row(ln_gain), row(layer_scale), row(b_down), pbias
+        pn, pb, keep_up, keep_down, got_up, got_down, img, gout, std, inv, dww, row(ln_gain), row(layer_scale), row(b_down), pbias
     )
     shard = lax.axis_index("fsdp")
     grad_b_up = lax.dynamic_slice(small[54:56].reshape(-1), (shard * HID,), (HID,)).astype(BF16)

time: 301 us -> 278 us (0.924)
  matrix products: 48.6 us -> 0 us
  Pallas kernels: 212 us -> 258 us
  other arithmetic: 17.3 us -> 0.01 us
    dot_general x12 -> x0, matrix products: 48.6 us -> none  [the longest x2 10.8 us: mlp(): lax.dot_general(grad_pre, wu, nt, preferred_element_type=F32)]
    pallas_call x1, Pallas kernels: 69.8 us -> 111 us  [first_call(): pl.pallas_call(first_kernel, out_shape=(jax.ShapeDtypeStruct((ROWS, CH),...]
    another operation x3 -> x0, other arithmetic: 17.3 us -> none  [the longest x1 8.43 us: mlp(): jnp.stack(ups)]
    pallas_call x1, Pallas kernels: 142 us -> 147 us  [second_call(): pl.pallas_call(second_kernel, out_shape=(jax.ShapeDtypeStruct((ROWS, CH),...]
    unnamed x64 -> x12, local copies, waits for them, and re-layouts: 15.7 us -> 11.5 us
where the time goes in v2:
time: 278 us
  Pallas kernels  258 us (93%)
  local copies, waits for them, and re-layouts  19.5 us (7%)
    pallas_call x1, Pallas kernels, second_call(): pl.pallas_call(second_kernel, out_shape=(jax.ShapeDtypeStruct((ROWS, CH),...  147 us
    pallas_call x1, Pallas kernels, first_call(): pl.pallas_call(first_kernel, out_shape=(jax.ShapeDtypeStruct((ROWS, CH),...  111 us
    unnamed x12, local copies, waits for them, and re-layouts  11.5 us

profile of v2, /device:TPU:1, one launch (start us, length us, event | category | flops | bytes accessed | tf_op | source)
XLA Modules:
  0.0 278.1 jit_solution(5863375521715747770)
XLA Ops:
  0.6 2.0 reshape.64.dww
  2.7 1.3 broadcast_in_dim.2.bu
  4.0 111.3 %shard_map.194 = (f32[128,3072]{1,0:T(8,128)}, f32[128,128]{1,0:T(8,128)}, bf16[512,3072]{1,0:T(8,128)(2,1)}, bf16[512,3072]{1,0:T(8,128)(2,1)}, bf16[3072,768]{...) custom-call(bf16[128,3072]{1,0:T(8,128)(2,1)} %bitcast.19, ...), custom_call_target="tpu_custom_call" | custom-call | tf_op jit(solution)/shard_map/pallas_call | solution.py:431
  115.3 146.7 %shard_map.195 = (bf16[128,3072]{1,0:T(8,128)(2,1)}, bf16[128,3072]{1,0:T(8,128)(2,1)}, bf16[3072,768]{1,0:T(8,128)(2,1)}, bf16[768,3072]{1,0:T(8,128)(2,1)}, f32[64,3072]{1,0:T(8,128)}) custom-call(bf16[512,3072]{1,0:T(8,128)(2,1)} %get-tuple-element.25.pn, bf16[512,3072]{1,0:T(8,128)(2,1)} %get-tuple-element.26.pb, ...), custom_call_target="tpu_custom_call" | custom-call | tf_op jit(solution)/shard_map/pallas_call | solution.py:894
  261.9 0.0 copy-start
  261.9 1.2 slice.22
  263.2 0.9 reshape.73
  264.1 1.8 fusion
  265.9 0.9 slice_bitcast_fusion
  266.8 0.7 dynamic_slice.5
  267.5 2.1 copy.27
  269.5 0.0 copy-done
  269.5 0.0 slice-start
  269.6 0.9 copy.28
  270.4 0.0 slice-start.1
  270.4 5.5 %copy.29 = bf16[3072,768]{1,0:T(8,128)(2,1)} copy(bf16[3072,768]{1,0:T(8,128)(2,1)} %get-tuple-element.57) | data formatting | bytes 9437184
  275.9 0.0 slice-done
  275.9 0.0 slice-done.1
  275.9 2.2 copy.30
  (2 shorter events, 0.0 us)
Async XLA Ops:
  261.9 7.6 %copy-start = (bf16[128,3072]{1,0:T(8,128)(2,1)S(1)}, bf16[128,3072]{1,0:T(8,128)(2,1)}, u32[]{:S(2)}) copy-start(bf16[128,3072]{1,0:T(8,128)(2,1)} %get-tuple-element.35) | copy-start | bytes 2359300
  269.5 6.4 %slice-start = ((s8[4718592]{0:T(1024)(128)(4,1)}), s8[4194304]{0:T(1024)(128)(4,1)S(1)}, s32[]{:S(2)}) async-start(s8[4718592]{0:T(1024)(128)(4,1)} %bitcast.17), calls=%async_computation | async-start | bytes 8388608
  270.4 5.5 %slice-start.1 = ((s8[4718592]{0:T(1024)(128)(4,1)}), s8[524288]{0:T(1024)(128)(4,1)S(1)}, s32[]{:S(2)}) async-start(s8[4718592]{0:T(1024)(128)(4,1)} %bitcast.17), calls=%async_computation.1 | async-start | bytes 1048576

commit v3 on v2

--- a/solution.py
+++ b/solution.py
@@ -122,8 +122,7 @@
     for horizontal in range(7):
         moved = [shifted(tile, horizontal - 3) for tile in pixels]
         for vertical in range(7):
-            tap = vertical * 7 + horizontal
-            weight = jnp.broadcast_to(dww[tap : tap + 1, cs], (8, LANES))
+            weight = jnp.broadcast_to(dww[vertical, horizontal : horizontal + 1, cs], (8, LANES))
             for image in range(2):
                 for p in range(8):
                     source = p + vertical - 3
@@ -144,8 +143,8 @@
 
 def first_kernel(
     img, gout, dww, dwb, gain, shift, lscale, wu, wd, bu,
-    std, inv, pn, pb, keep_up, keep_down, got_up, got_down, bias_sums,
-    gn, gs, wuv, wdv, bo, hid, gp, keep32, pnv, pbv, up_v, down_v,
+    std, inv, pn, pb, keep_up, keep_down, got_up, got_down, bias_sums, scale_sums,
+    gn, gs, wuv, wdv, b_own, bo, hid, gp, keep32, pnv, pbv, up_v, down_v,
     send, recv, local,
 ):
     me = Place()
@@ -156,24 +155,66 @@
     mate = me.at(core=me.other_core)
     wu_load = copies.here(wu, wuv.at[0])
     wd_load = copies.here(wd, wdv.at[0])
-    greet([right, left, cut, pair, mate])
-
-    up_rows, down_rows, parts = 192, 48, 4
-    theirs = (1 - me.x_lo) * 2 + me.core
-    mine = me.x_lo * 2 + me.core
-    pairs = (1 - me.x_lo) * 2 + me.core
+    b_own[...] = jnp.broadcast_to(bu[...], (8, HID))
+    z_right_chip, z_left_chip, z, z_right, z_left, z_far = me.ring("z")
+    greet([right, left, cut, pair, mate, z_right_chip, z_left_chip])
+
     weights = (wuv.at[1], wdv.at[1])
-
-    def chunk(matrix, quarter, part):
-        size = up_rows if matrix == 0 else down_rows
-        return rows_at(quarter * (size * parts) + part * size, size)
-
-    order = [(m, k) for m in range(2) for k in range(parts)]
-    bias = copies.push(bu, bo, cut)
+    sizes = (192, 48)
+    sides = (me.x_lo, 1 - me.x_lo)
+
+    def piece(m, side, which):
+        return rows_at((side * 8 + which * 2 + me.core) * sizes[m], sizes[m])
+
+    def held(m, k, which):
+        return weights[m].at[piece(m, sides[k], which)]
+
+    bias = copies.push(b_own, bo, cut)
     over_cut = []
-    for m, k in order:
-        at = chunk(m, theirs, k)
+    for m in range(2):
+        at = piece(m, sides[1], z)
         over_cut.append(copies.push((wu, wd)[m].at[at], weights[m].at[at], cut))
+    swapped, ring_one, ring_two, mates = {}, {}, {}, {0: [], 1: []}
+
+    def to_mate(m, ref):
+        mates[m].append(copies.push(ref, ref, mate))
+
+    def around(m, k):
+        ref = held(m, k, z)
+        ring_one[m, k] = copies.push(ref, ref, z_right_chip), copies.push(ref, ref, z_left_chip)
+        to_mate(m, ref)
+
+    def from_cut(m):
+        over_cut[m].wait_recv()
+        ref = held(m, 0, z)
+        swapped[m] = copies.push(ref, ref, pair)
+        around(m, 0)
+
+    def from_pair(m):
+        swapped[m].wait_recv()
+        around(m, 1)
+
+    def from_ring(m, k):
+        width = (HID, CH)[m] // 2
+        ring_one[m, k][0].wait_recv()
+        ref = held(m, k, z_left)
+        part = weights[m].at[piece(m, sides[k], z_left), pl.ds(0, width)]
+        one = copies.push(part, part, z_right_chip)
+        to_mate(m, ref)
+        ring_one[m, k][1].wait_recv()
+        ref = held(m, k, z_right)
+        part = weights[m].at[piece(m, sides[k], z_right), pl.ds(width, width)]
+        ring_two[m, k] = one, copies.push(part, part, z_left_chip)
+        to_mate(m, ref)
+
+    def from_far(m, k):
+        for copy in ring_two[m, k]:
+            copy.wait_recv()
+        to_mate(m, held(m, k, z_far))
+
+    def arrived(m):
+        for copy in mates[m]:
+            copy.wait_recv()
 
     own = rows_at(y * ROWS, ROWS)
 
@@ -203,27 +244,6 @@
         to_left = copies.push(buffer.at[high], buffer.at[high], left)
         return [to_right, to_left]
 
-    relayed, last = {}, {}
-
-    def relay(index):
-        m, k = order[index]
-        over_cut[index].wait_recv()
-        at = chunk(m, mine, k)
-        ref = weights[m].at[at]
-        relayed[index] = copies.push(ref, ref, pair), copies.push(ref, ref, mate)
-
-    def relay_pair(index):
-        m, k = order[index]
-        relayed[index][0].wait_recv()
-        at = chunk(m, pairs, k)
-        ref = weights[m].at[at]
-        last[index] = copies.push(ref, ref, mate)
-
-    def arrived(indices):
-        for index in indices:
-            relayed[index][1].wait_recv()
-            last[index].wait_recv()
-
     s_first, s_second = spread(gs)
 
     def conv_step(block, carry):
@@ -231,7 +251,7 @@
         return carry
 
     lax.fori_loop(0, BLOCKS // 2, conv_step, 0)
-    relay(0)
+    from_cut(0)
     lax.fori_loop(BLOCKS // 2, BLOCKS, conv_step, 0)
 
     def add_block(block, total):
@@ -257,8 +277,8 @@
 
     lax.fori_loop(0, BLOCKS, norm_block, 0)
     n_first, n_second = spread(gn)
-    relay(1)
     s_last = forward(s_first, gs)
+    from_cut(1)
 
     tile = 256
 
@@ -267,26 +287,33 @@
 
     bias_sums[...] = jnp.zeros_like(bias_sums)
 
+    def own_grad_hidden():
+        def body(index, carry):
+            cs = hidden_tile(index)
+            keep32[0, :, cs] = lax.dot_general(gs[...], wdv[0, cs, :], NT, preferred_element_type=F32)
+            return carry
+
+        lax.fori_loop(0, HID // tile, body, 0)
+
     def up_rows_of(s, position):
         at = rows_at(position * ROWS, ROWS)
-
+        pre = jnp.dot(gn[at, :], wuv[s], preferred_element_type=F32)
+        value, slope = gelu_parts(pre + (b_own if s == 0 else bo)[0:1, :])
+        hid[s, at, :] = value.astype(BF16)
+        if s == 0:
+            grad = (keep32[0, at, :] * slope).astype(BF16)
+            gp[0, at, :] = grad
+            bias_sums[0:1, :] = bias_sums[0:1, :] + jnp.sum(grad.astype(F32), axis=0, keepdims=True)
+        else:
+            keep32[1, at, :] = slope
+
+    def other_grad():
         def body(index, carry):
             cs = hidden_tile(index)
-            pre = jnp.dot(gn[at, :], wuv[s, :, cs], preferred_element_type=F32)
-            value, slope = gelu_parts(pre + (bu if s == 0 else bo)[0:1, cs])
-            hid[s, at, cs] = value.astype(BF16)
-            keep32[s, at, cs] = slope
-            return carry
-
-        lax.fori_loop(0, HID // tile, body, 0)
-
-    def grad_of(s):
-        def body(index, carry):
-            cs = hidden_tile(index)
-            grad = lax.dot_general(gs[...], wdv[s, cs, :], NT, preferred_element_type=F32)
-            pre = (grad * keep32[s, :, cs]).astype(BF16)
-            gp[s, :, cs] = pre
-            bias_sums[s : s + 1, cs] = jnp.sum(pre.astype(F32), axis=0, keepdims=True)
+            grad = lax.dot_general(gs[...], wdv[1, cs, :], NT, preferred_element_type=F32)
+            pre = (grad * keep32[1, :, cs]).astype(BF16)
+            gp[1, :, cs] = pre
+            bias_sums[1:2, cs] = jnp.sum(pre.astype(F32), axis=0, keepdims=True)
             return carry
 
         lax.fori_loop(0, HID // tile, body, 0)
@@ -333,87 +360,76 @@
         for part in range(4):
             if s == 1:
                 placed(0, 0, part)
-
-            def body(index, carry, part=part):
-                rows = pl.ds(pl.multiple_of(part * 768 + index * tile, tile), tile)
-                up_v[rows, :] = lax.dot_general(gn[:, rows], gp[s], TN, preferred_element_type=F32).astype(BF16)
-                return carry
-
-            lax.fori_loop(0, 768 // tile, body, 0)
+            rows = pl.ds(part * 768, 768)
+            up_v[rows, :] = lax.dot_general(gn[:, rows], gp[s], TN, preferred_element_type=F32).astype(BF16)
             place(0, s, part)
 
     def part_down(s):
         for part in range(4):
             if s == 1:
                 placed(1, 0, part)
-
-            def body(index, carry, part=part):
-                cs = pl.ds(pl.multiple_of(part * 768 + index * tile, tile), tile)
-                down_v[:, cs] = lax.dot_general(hid[s], gs[:, cs], TN, preferred_element_type=F32).astype(BF16)
-                return carry
-
-            lax.fori_loop(0, 768 // tile, body, 0)
+            cs = pl.ds(part * 768, 768)
+            down_v[:, cs] = lax.dot_general(hid[s], gs[:, cs], TN, preferred_element_type=F32).astype(BF16)
             place(1, s, part)
 
+    from_pair(0)
+    from_ring(0, 0)
+    from_pair(1)
+    from_ring(0, 1)
     wu_load.wait()
-    relay(2)
-    relay_pair(0)
+    wd_load.wait()
+    for copy in s_second + s_last:
+        copy.wait_recv()
+    own_grad_hidden()
+    from_ring(1, 0)
+    from_ring(1, 1)
+    n_last = forward(n_first, gn)
     up_rows_of(0, y)
-    relay_pair(1)
-    relay(3)
-    relay_pair(2)
-    n_last = forward(n_first, gn)
-    relay(4)
-    relay_pair(3)
+    from_far(0, 0)
+    from_far(0, 1)
+    bias.wait_recv()
     for copy in n_second:
         copy.wait_recv()
     up_rows_of(0, y_right)
     up_rows_of(0, y_left)
-    relay(5)
-    relay_pair(4)
-    bias.wait_recv()
-    arrived(range(4))
+    from_far(1, 0)
+    from_far(1, 1)
+    arrived(0)
     up_rows_of(1, y)
     up_rows_of(1, y_right)
-    relay(6)
-    relay_pair(5)
     up_rows_of(1, y_left)
-    wd_load.wait()
-    for copy in s_second + s_last:
-        copy.wait_recv()
-    relay(7)
-    relay_pair(6)
     for copy in n_last:
         copy.wait_recv()
     up_rows_of(0, y_far)
-    relay_pair(7)
-    grad_of(0)
     up_rows_of(1, y_far)
+    part_down(0)
     part_up(0)
-    part_down(0)
-    arrived(range(4, 8))
-    grad_of(1)
+    part_down(1)
+    arrived(1)
+    other_grad()
     part_up(1)
-    part_down(1)
+    wide = 768
 
     def normed_back(index, carry):
-        cs = pl.ds(pl.multiple_of(index * tile, tile), tile)
+        cs = pl.ds(pl.multiple_of(index * wide, wide), wide)
         total = lax.dot_general(gp[0], wuv[0, cs, :], NT, preferred_element_type=F32)
         total = total + lax.dot_general(gp[1], wuv[1, cs, :], NT, preferred_element_type=F32)
         pnv[:, cs] = total.astype(BF16)
         return carry
 
-    lax.fori_loop(0, CH // tile, normed_back, 0)
+    lax.fori_loop(0, CH // wide, normed_back, 0)
     pn_out = copies.here(pnv, pn)
 
     def branch_tile(index, carry):
-        cs = pl.ds(pl.multiple_of(index * tile, tile), tile)
+        cs = pl.ds(pl.multiple_of(index * wide, wide), wide)
         total = jnp.dot(hid[0], wdv[0, :, cs], preferred_element_type=F32)
         total = total + jnp.dot(hid[1], wdv[1, :, cs], preferred_element_type=F32)
         pbv[:, cs] = total.astype(BF16)
+        product = jnp.sum(total * gs[:, cs].astype(F32), axis=0, keepdims=True)
+        scale_sums[0:1, cs] = product / lscale[0:1, cs]
         return carry
 
-    lax.fori_loop(0, CH // tile, branch_tile, 0)
+    lax.fori_loop(0, CH // wide, branch_tile, 0)
     pb_out = copies.here(pbv, pb)
 
     pn_out.wait()
@@ -426,7 +442,7 @@
 
 
 def first_call(img, gout, dww, dwb, gain, shift, lscale, wu, wd, bu):
-    remote = 56
+    remote = 64
     rows = 4 * ROWS
     return pl.pallas_call(
         first_kernel,
@@ -440,14 +456,16 @@
             jax.ShapeDtypeStruct((CH, HID), BF16),
             jax.ShapeDtypeStruct((HID, CH), BF16),
             jax.ShapeDtypeStruct((8, HID), F32),
+            jax.ShapeDtypeStruct((8, CH), F32),
         ),
         in_specs=[VMEM] * 7 + [ANY, ANY, VMEM],
-        out_specs=(VMEM, VMEM, ANY, ANY, ANY, ANY, ANY, ANY, VMEM),
+        out_specs=(VMEM, VMEM, ANY, ANY, ANY, ANY, ANY, ANY, VMEM, VMEM),
         scratch_shapes=[
             pltpu.VMEM((rows, CH), BF16),
             pltpu.VMEM((rows, CH), BF16),
             pltpu.VMEM((2, CH, HID), BF16),
             pltpu.VMEM((2, HID, CH), BF16),
+            pltpu.VMEM((8, HID), F32),
             pltpu.VMEM((8, HID), F32),
             pltpu.VMEM((2, rows, HID), BF16),
             pltpu.VMEM((2, rows, HID), BF16),
@@ -490,22 +508,31 @@
         return self.base + which * self.rows
 
     def begin(self):
-        at = rows_at(self.block(self.at_far), self.rows) if self.step == 16 else pl.ds(self.block(self.at_far), self.rows)
+        at = rows_at(self.block(self.at_far), self.rows)
         h = self.half
         self.one = [
             self.copies.push(self.data.at[at, pl.ds(0, h)], self.far.at[0], self.right),
             self.copies.push(self.data.at[at, pl.ds(h, h)], self.far.at[1], self.left),
         ]
 
+    def sides(self):
+        return enumerate(((self.right, self.at_right), (self.left, self.at_left)))
+
+    def own_halves(self):
+        h = self.half
+        self.two = []
+        for side, (device, block) in self.sides():
+            at, cs = rows_at(self.block(block), self.rows), pl.ds((1 - side) * h, h)
+            self.two.append(self.copies.push(self.data.at[at, cs], self.near.at[side, :, cs], device))
+
     def middle(self):
         h = self.half
-        self.two = []
-        for side, (device, block) in enumerate(((self.right, self.at_right), (self.left, self.at_left))):
+        for side, (device, block) in self.sides():
             self.one[side].wait_recv()
             start = self.block(block)
             add_rows(self.data, start, [(self.far.at[side], 0, 0)], self.rows, side * h, h, self.step)
-            at = rows_at(start, self.rows)
-            self.two.append(self.copies.push(self.data.at[at], self.near.at[side], device))
+            at, cs = rows_at(start, self.rows), pl.ds(side * h, h)
+            self.two.append(self.copies.push(self.data.at[at, cs], self.near.at[side, :, cs], device))
 
     def end(self):
         for copy in self.two:
@@ -529,7 +556,7 @@
 
 
 def second_kernel(
-    pn, pb, gu, gd, ru, rd, img, gout, std, inv, dww, gain, lscale, bdown, pbias,
+    pn, pb, gu, gd, ru, rd, img, gout, std, inv, dww, gain, lscale, bdown, pbias, pscale,
     out_img, grad_img, out_up, out_down, out_small,
     guv, gdv, cu, cd, d1a, d1b, u1a, u1b, d2a, d2b, u2a, u2b, tq, fd, fu,
     nv, bv, n1, n2, b1, b2, gcv, sm, smc, sya, syb, sx, sz, smo,
@@ -541,7 +568,6 @@
     mate = me.at(core=me.other_core)
     x_cut = me.at(x=me.x_cut)
     x_pair = me.at(x=me.x_pair)
-    greet([ring_x[0], ring_x[1], ring_y[0], ring_y[1], ring_z[0], ring_z[1], mate])
     x, y, z = me.x, me.y, me.z
     factor = 1.0 / math.sqrt(16384.0)
 
@@ -549,6 +575,7 @@
     x_far, x_right, x_left = ring_x[5], ring_x[3], ring_x[4]
     order = [(0, z_far), (1, x_far), (0, z_right), (1, x_right), (0, z_left), (1, x_left), (0, z), (1, x)]
     swaps, loads = [], []
+    load_n = copies.here(pn, nv)
 
     def piece(matrix, which):
         return rows_at(which * 192, 192) if matrix == 0 else rows_at(which * 768, 768)
@@ -558,14 +585,14 @@
         at = piece(m, which)
         swaps.append(copies.here(got.at[at], dst.at[at]))
         loads.append(copies.here(src.at[at], mine.at[at]))
+    load_b = copies.here(pb, bv)
+    greet([ring_x[0], ring_x[1], ring_y[0], ring_y[1], ring_z[0], ring_z[1], mate])
 
     y_far = ring_y[5]
-    load_n = copies.here(pn, nv)
-    load_b = copies.here(pb, bv)
     load_n.wait()
     rs_n = RingSum(copies, ring_y, nv, 0, ROWS, n2, n1)
     rs_n.begin()
-    load_b.wait()
+    rs_n.own_halves()
     rs_b = RingSum(copies, ring_y, bv, 0, ROWS, b2, b1)
 
     def merge(index):
@@ -582,15 +609,16 @@
     rs_d1.begin()
     merge(1)
     rs_u1.begin()
+    for index in range(2, 6):
+        merge(index)
+    rs_d1.own_halves()
+    rs_u1.own_halves()
+    load_b.wait()
     rs_b.begin()
-    merge(2)
-    merge(3)
     rs_n.middle()
-    merge(4)
-    merge(5)
+    rs_b.own_halves()
     rs_d1.middle()
     rs_u1.middle()
-    rs_b.middle()
     merge(6)
     merge(7)
 
@@ -629,13 +657,6 @@
 
     lax.fori_loop(0, BLOCKS, norm_apply, 0)
 
-    rs_d1.end()
-    rs_d2 = RingSum(copies, ring_x, gdv, z * 192, 48, d2b, d2a)
-    rs_d2.begin()
-    rs_u1.end()
-    rs_u2 = RingSum(copies, ring_z, guv, x * 768, 192, u2b, u2a)
-    rs_u2.begin()
-
     def conv_back(block, carry):
         cs = lanes_at(block)
         pixels = tile_rows(img, block)
@@ -646,7 +667,7 @@
             moved = [shifted(tile, 3 - horizontal) for tile in grads]
             for vertical in range(7):
                 tap = vertical * 7 + horizontal
-                weight = jnp.broadcast_to(dww[tap : tap + 1, cs], (8, LANES))
+                weight = jnp.broadcast_to(dww[vertical, horizontal : horizontal + 1, cs], (8, LANES))
                 taps = jnp.zeros((8, LANES), F32)
                 for image in range(2):
                     for p in range(8):
@@ -662,21 +683,13 @@
 
     lax.fori_loop(0, BLOCKS, conv_back, 0)
 
-    rs_d2.middle()
-    rs_u2.middle()
-
-    rs_b.end()
-
-    def result_block(block, carry):
+    def scale_block(block, carry):
         cs = lanes_at(block)
-        branch = own_rows(bv, cs) + bdown[0:1, cs]
-        upstream = gout[:, cs].astype(F32)
-        sm[53:54, cs] = jnp.sum(upstream * branch, axis=0, keepdims=True)
-        out_img[:, cs] = (img[:, cs].astype(F32) + lscale[0:1, cs] * branch).astype(BF16)
+        upstream = jnp.sum(gout[:, cs].astype(F32), axis=0, keepdims=True)
+        sm[53:54, cs] = pscale[0:1, cs] + upstream * bdown[0:1, cs]
         return carry
 
-    lax.fori_loop(0, BLOCKS, result_block, 0)
-
+    lax.fori_loop(0, BLOCKS, scale_block, 0)
     sm[54:64, :] = jnp.zeros((10, CH), F32)
     for s in range(2):
         shard = y * 2 + (me.x_hi if s == 0 else 1 - me.x_hi)
@@ -688,63 +701,52 @@
                 sm[54 + line : 55 + line, at] = pbias[s : s + 1, :]
 
     swap_small = copies.push(sm.at[pl.ds(pl.multiple_of(me.other_core * 32, 8), 32)], smc, mate)
-
-    rs_d2.end()
-    rs_u2.end()
-    at_d = z * 192 + x * 48
-    at_u = x * 768 + z * 192
-    fd[...] = (gdv[rows_at(at_d, 48), :].astype(F32) * factor).astype(BF16)
-    fu[...] = (guv[rows_at(at_u, 192), :].astype(F32) * factor).astype(BF16)
-    needed = me.x_hi == me.core
-
+    small_rows = me.core * 32
+    sm_at = pl.ds(pl.multiple_of(small_rows, 8), 32)
+    yr, yl, yy, y_right, y_left, y_far = ring_y
     zr, zl = ring_z[0], ring_z[1]
-
-    def slot(which):
-        return rows_at(which * 192, 192)
-
-    tq_own = copies.here(fu, tq.at[slot(z)])
-    up_one = [copies.push(fu, tq.at[slot(z)], zr), copies.push(fu, tq.at[slot(z)], zl)]
-
-    def drow(which_x, which_z=None):
-        return rows_at((z if which_z is None else which_z) * 192 + which_x * 48, 48)
-
-    d_cut = copies.remote(fd, out_down.at[drow(x)], x_cut)
-    d_swap = copies.remote(fd, out_down.at[drow(x)], x_pair)
-    d_cut_swap = copies.remote(out_down.at[drow(me.x_cut)], out_down.at[drow(me.x_cut)], x_pair)
-
-    @pl.when(jnp.logical_not(needed))
-    def _():
-        d_cut.start()
-
-    d_own = pltpu.make_async_copy(fd, out_down.at[drow(x)], local.at[30])
-
-    @pl.when(needed)
-    def _():
-        d_own.start()
-        d_swap.start()
-
-    small_rows = me.core * 32
-    swap_small.wait_recv()
-    sm_at = pl.ds(pl.multiple_of(small_rows, 8), 32)
-    sm[sm_at, :] = sm[sm_at, :] + smc[...]
-
-    yr, yl, yy, y_right, y_left, y_far = ring_y
+    h = CH // 2
+    lo, hi = pl.ds(0, h), pl.ds(h, h)
 
     def small_piece(which):
         return pl.ds(pl.multiple_of(small_rows + which * 8, 8), 8)
 
-    h = CH // 2
+    def all_begin(buffer, ring):
+        where = ring[2]
+        return [
+            copies.push(buffer.at[where], buffer.at[where], ring[0]),
+            copies.push(buffer.at[where], buffer.at[where], ring[1]),
+        ]
+
+    def all_middle(buffer, ring, one):
+        at_right, at_left = ring[3], ring[4]
+        one[0].wait_recv()
+        two = [copies.push(buffer.at[at_left, :, lo], buffer.at[at_left, :, lo], ring[0])]
+        one[1].wait_recv()
+        two.append(copies.push(buffer.at[at_right, :, hi], buffer.at[at_right, :, hi], ring[1]))
+        return two
+
+    def all_end(buffer, two):
+        for copy in two:
+            copy.wait_recv()
+        return buffer[0] + buffer[1] + buffer[2] + buffer[3]
+
+    rs_b.middle()
+    swap_small.wait_recv()
+    sm[sm_at, :] = sm[sm_at, :] + smc[...]
     s_one = [
-        copies.push(sm.at[small_piece(y_far), pl.ds(0, h)], sya.at[0], yr),
-        copies.push(sm.at[small_piece(y_far), pl.ds(h, h)], sya.at[1], yl),
+        copies.push(sm.at[small_piece(y_far), lo], sya.at[0], yr),
+        copies.push(sm.at[small_piece(y_far), hi], sya.at[1], yl),
     ]
 
-    up_one[0].wait_recv()
-    z_left_slot, z_right_slot = slot(z_left), slot(z_right)
-    hu = HID // 2
-    up_two = [copies.push(tq.at[z_left_slot, pl.ds(0, hu)], tq.at[z_left_slot, pl.ds(0, hu)], zr)]
-    up_one[1].wait_recv()
-    up_two.append(copies.push(tq.at[z_right_slot, pl.ds(hu, hu)], tq.at[z_right_slot, pl.ds(hu, hu)], zl))
+    rs_d1.end()
+    rs_d2 = RingSum(copies, ring_x, gdv, z * 192, 48, d2b, d2a)
+    rs_d2.begin()
+    rs_d2.own_halves()
+    rs_u1.end()
+    rs_u2 = RingSum(copies, ring_z, guv, x * 768, 192, u2b, u2a)
+    rs_u2.begin()
+    rs_u2.own_halves()
 
     s_two = []
     for side, (device, which) in enumerate(((yr, y_right), (yl, y_left))):
@@ -752,34 +754,88 @@
         at = small_piece(which)
         sm[at, pl.ds(side * h, h)] = sm[at, pl.ds(side * h, h)] + sya[side]
         s_two.append(copies.push(sm.at[at], syb.at[side], device))
+    rs_d2.middle()
+    rs_u2.middle()
+    for side in range(2):
+        s_two[side].wait_recv()
+    at = small_piece(yy)
+    sx[pl.ds(x, 1)] = (sm[at, :] + syb[0] + syb[1])[None]
+    sx_one = all_begin(sx, ring_x)
+
+    rs_d2.end()
+    at_d = z * 192 + x * 48
+    at_u = x * 768 + z * 192
+    fd[...] = (gdv[rows_at(at_d, 48), :].astype(F32) * factor).astype(BF16)
+    needed = me.x_hi == me.core
+
+    def drow(which_x):
+        return rows_at(z * 192 + which_x * 48, 48)
+
+    d_cut = copies.remote(fd, out_down.at[drow(x)], x_cut)
+    d_swap = copies.remote(fd, out_down.at[drow(x)], x_pair)
+    d_cut_swap = copies.remote(out_down.at[drow(me.x_cut)], out_down.at[drow(me.x_cut)], x_pair)
+    d_own = pltpu.make_async_copy(fd, out_down.at[drow(x)], local.at[30])
+
+    @pl.when(jnp.logical_not(needed))
+    def _():
+        d_cut.start()
+
+    @pl.when(needed)
+    def _():
+        d_own.start()
+        d_swap.start()
+
+    rs_u2.end()
+    fu[...] = (guv[rows_at(at_u, 192), :].astype(F32) * factor).astype(BF16)
+
+    def slot(which):
+        return rows_at(which * 192, 192)
+
+    tq_own = copies.here(fu, tq.at[slot(z)])
+    up_one = [copies.push(fu, tq.at[slot(z)], zr), copies.push(fu, tq.at[slot(z)], zl)]
+    sx_two = all_middle(sx, ring_x, sx_one)
+
+    rs_b.end()
+
+    def result_block(block, carry):
+        cs = lanes_at(block)
+        branch = own_rows(bv, cs) + bdown[0:1, cs]
+        out_img[:, cs] = (img[:, cs].astype(F32) + lscale[0:1, cs] * branch).astype(BF16)
+        return carry
+
+    lax.fori_loop(0, BLOCKS, result_block, 0)
 
     @pl.when(needed)
     def _():
         d_cut.wait_recv()
         d_cut_swap.start()
 
-    for side in range(2):
-        s_two[side].wait_recv()
-    at = small_piece(yy)
-    sx[pl.ds(x, 1)] = (sm[at, :] + syb[0] + syb[1])[None]
-
-    def small_all(buffer, ring):
-        to_right, to_left, where, _, at_left, _ = ring[0], ring[1], ring[2], ring[3], ring[4], ring[5]
-        at_right = ring[3]
-        one = [
-            copies.push(buffer.at[where], buffer.at[where], to_right),
-            copies.push(buffer.at[where], buffer.at[where], to_left),
-        ]
-        one[0].wait_recv()
-        lo, hi = pl.ds(0, h), pl.ds(h, h)
-        two = [copies.push(buffer.at[at_left, :, lo], buffer.at[at_left, :, lo], to_right)]
-        one[1].wait_recv()
-        two.append(copies.push(buffer.at[at_right, :, hi], buffer.at[at_right, :, hi], to_left))
-        for copy in two:
-            copy.wait_recv()
-        return buffer[0] + buffer[1] + buffer[2] + buffer[3]
-
-    sz[pl.ds(z, 1)] = small_all(sx, ring_x)[None]
+    sz[pl.ds(z, 1)] = all_end(sx, sx_two)[None]
+    sz_one = all_begin(sz, ring_z)
+    hu = HID // 2
+    z_left_slot, z_right_slot = slot(z_left), slot(z_right)
+    up_one[0].wait_recv()
+    up_two = [copies.push(tq.at[z_left_slot, pl.ds(0, hu)], tq.at[z_left_slot, pl.ds(0, hu)], zr)]
+    up_one[1].wait_recv()
+    up_two.append(copies.push(tq.at[z_right_slot, pl.ds(hu, hu)], tq.at[z_right_slot, pl.ds(hu, hu)], zl))
+    sz_two = all_middle(sz, ring_z, sz_one)
+
+    def dblock(which):
+        return rows_at(which * 192, 192)
+
+    block = dblock(z)
+    d_right = copies.remote(out_down.at[block], out_down.at[block], zr)
+    d_left = copies.remote(out_down.at[block], out_down.at[block], zl)
+    d_mate = copies.remote(out_down.at[block], out_down.at[block], mate)
+
+    @pl.when(needed)
+    def _():
+        d_own.wait()
+        d_swap.wait_recv()
+        d_cut_swap.wait_recv()
+        d_right.start()
+        d_left.start()
+        d_mate.start()
 
     for copy in up_two:
         copy.wait_recv()
@@ -803,36 +859,23 @@
         u_mate.start()
         u_own.start()
 
-    total = small_all(sz, ring_z)
+    total = all_end(sz, sz_two)
     smo_at = small_piece(yy)
     smo[smo_at, :] = total * factor
-
-    def small_back():
-        one = [
-            copies.push(smo.at[smo_at], smo.at[smo_at], yr),
-            copies.push(smo.at[smo_at], smo.at[smo_at], yl),
-        ]
-        lo, hi = pl.ds(0, h), pl.ds(h, h)
-        from_left, from_right = small_piece(y_left), small_piece(y_right)
-        one[0].wait_recv()
-        two = [copies.push(smo.at[from_left, lo], smo.at[from_left, lo], yr)]
-        one[1].wait_recv()
-        two.append(copies.push(smo.at[from_right, hi], smo.at[from_right, hi], yl))
-        for copy in two:
-            copy.wait_recv()
-        return copies.push(smo.at[sm_at], smo.at[sm_at], mate)
-
-    small_mate = small_back()
-
-    def dblock(which):
-        return rows_at(which * 192, 192)
-
-    hd = CH // 2
-    lo, hi = pl.ds(0, hd), pl.ds(hd, hd)
-    block, block_l, block_r, block_f = dblock(z), dblock(z_left), dblock(z_right), dblock(z_far)
-    d_right = copies.remote(out_down.at[block], out_down.at[block], zr)
-    d_left = copies.remote(out_down.at[block], out_down.at[block], zl)
-    d_mate = copies.remote(out_down.at[block], out_down.at[block], mate)
+    so_one = [
+        copies.push(smo.at[smo_at], smo.at[smo_at], yr),
+        copies.push(smo.at[smo_at], smo.at[smo_at], yl),
+    ]
+    from_left, from_right = small_piece(y_left), small_piece(y_right)
+    so_one[0].wait_recv()
+    so_two = [copies.push(smo.at[from_left, lo], smo.at[from_left, lo], yr)]
+    so_one[1].wait_recv()
+    so_two.append(copies.push(smo.at[from_right, hi], smo.at[from_right, hi], yl))
+    for copy in so_two:
+        copy.wait_recv()
+    small_mate = copies.push(smo.at[sm_at], smo.at[sm_at], mate)
+
+    block_l, block_r, block_f = dblock(z_left), dblock(z_right), dblock(z_far)
     d_fwd_right = copies.remote(out_down.at[block_l, lo], out_down.at[block_l, lo], zr)
     d_fwd_left = copies.remote(out_down.at[block_r, hi], out_down.at[block_r, hi], zl)
     d_mate_l = copies.remote(out_down.at[block_l], out_down.at[block_l], mate)
@@ -846,12 +889,6 @@
 
     @pl.when(needed)
     def _():
-        d_own.wait()
-        d_swap.wait_recv()
-        d_cut_swap.wait_recv()
-        d_right.start()
-        d_left.start()
-        d_mate.start()
         u_cut.wait_recv()
         u_cut_swap.start()
         u_mate_c.start()
@@ -888,7 +925,7 @@
 
 
 def second_call(*operands):
-    remote = 80
+    remote = 96
     bf = lambda *shape: pltpu.VMEM(shape, BF16)
     fl = lambda *shape: pltpu.VMEM(shape, F32)
     return pl.pallas_call(
@@ -900,7 +937,7 @@
             jax.ShapeDtypeStruct((HID, CH), BF16),
             jax.ShapeDtypeStruct((64, CH), F32),
         ),
-        in_specs=[ANY] * 6 + [VMEM] * 9,
+        in_specs=[ANY] * 6 + [VMEM] * 10,
         out_specs=(VMEM, VMEM, ANY, ANY, VMEM),
         scratch_shapes=[
             bf(CH, HID), bf(HID, CH), bf(CH, HID), bf(HID, CH),
@@ -921,34 +958,90 @@
     )(*operands)
 
 
+def last_kernel(oimg, gimg, up, down, small, o1, o2, o3, o4, dw, r1, r2, r3, r4, r5, gb, v1, v2, v3, v4, load, store):
+    trips = [(oimg, v1, o1), (gimg, v2, o2)]
+    for part in range(4):
+        rows = pl.ds(part * 768, 768)
+        trips.append((up.at[rows], v3.at[rows], o3.at[rows]))
+    for part in range(4):
+        rows = pl.ds(part * 192, 192)
+        trips.append((down.at[rows], v4.at[rows], o4.at[rows]))
+    loads = [pltpu.make_async_copy(src, mid, load.at[i]) for i, (src, mid, dst) in enumerate(trips)]
+    stores = [pltpu.make_async_copy(mid, dst, store.at[i]) for i, (src, mid, dst) in enumerate(trips)]
+    for move in loads:
+        move.start()
+    for vertical in range(7):
+        dw[vertical] = small[vertical * 7 : vertical * 7 + 7, :]
+    for index, ref in enumerate((r1, r2, r3, r4, r5)):
+        ref[...] = small[49 + index, :]
+    shard = lax.axis_index("fsdp")
+    at = pl.ds(pl.multiple_of(lax.rem(shard, 4) * HID, LANES), HID)
+    line = lax.div(shard, 4)
+    gb[...] = jnp.where(line == 0, small[54:55, at], small[55:56, at]).astype(BF16)
+    for first, second in zip(loads, stores):
+        first.wait()
+        second.start()
+    for move in stores:
+        move.wait()
+
+
+def last_call(oimg, gimg, up, down, small):
+    wide = jax.ShapeDtypeStruct((ROWS, CH), BF16)
+    line = jax.ShapeDtypeStruct((CH,), F32)
+    return pl.pallas_call(
+        last_kernel,
+        out_shape=(
+            wide,
+            wide,
+            jax.ShapeDtypeStruct((CH, HID), BF16),
+            jax.ShapeDtypeStruct((HID, CH), BF16),
+            jax.ShapeDtypeStruct((7, 7, CH), F32),
+            line,
+            line,
+            line,
+            line,
+            line,
+            jax.ShapeDtypeStruct((1, HID), BF16),
+        ),
+        in_specs=[ANY] * 4 + [VMEM],
+        out_specs=tuple([ANY] * 4 + [VMEM] * 7),
+        scratch_shapes=[
+            pltpu.VMEM((ROWS, CH), BF16),
+            pltpu.VMEM((ROWS, CH), BF16),
+            pltpu.VMEM((CH, HID), BF16),
+            pltpu.VMEM((HID, CH), BF16),
+            pltpu.SemaphoreType.DMA((10,)),
+            pltpu.SemaphoreType.DMA((10,)),
+        ],
+        compiler_params=pltpu.CompilerParams(vmem_limit_bytes=62 * 1024 * 1024),
+    )(oimg, gimg, up, down, small)
+
+
 def on_device(
     images, grad_out, dw_weight, dw_bias, ln_gain, ln_bias, w_up, b_up, w_down, b_down, layer_scale
 ):
     img = images.reshape(ROWS, CH)
     gout = grad_out.reshape(ROWS, CH)
-    dww = dw_weight.reshape(49, CH)
     row = lambda vector: vector.reshape(1, CH)
-    bu = jnp.broadcast_to(b_up.reshape(1, HID), (8, HID))
-    std, inv, pn, pb, keep_up, keep_down, got_up, got_down, pbias = first_call(
-        img, gout, dww, row(dw_bias), row(ln_gain), row(ln_bias), row(layer_scale), w_up, w_down, bu
+    std, inv, pn, pb, keep_up, keep_down, got_up, got_down, pbias, pscale = first_call(
+        img, gout, dw_weight, row(dw_bias), row(ln_gain), row(ln_bias), row(layer_scale), w_up, w_down, b_up.reshape(1, HID)
     )
     out_img, grad_img, out_up, out_down, small = second_call(
-        pn, pb, keep_up, keep_down, got_up, got_down, img, gout, std, inv, dww, row(ln_gain), row(layer_scale), row(b_down), pbias
+        pn, pb, keep_up, keep_down, got_up, got_down, img, gout, std, inv, dw_weight, row(ln_gain), row(layer_scale), row(b_down), pbias, pscale
     )
-    shard = lax.axis_index("fsdp")
-    grad_b_up = lax.dynamic_slice(small[54:56].reshape(-1), (shard * HID,), (HID,)).astype(BF16)
+    oimg, gimg, up, down, dw, r1, r2, r3, r4, r5, gb = last_call(out_img, grad_img, out_up, out_down, small)
     return (
-        out_img.reshape(images.shape),
-        grad_img.reshape(images.shape),
-        out_up,
-        grad_b_up,
-        out_down,
-        small[:49].reshape(dw_weight.shape),
-        small[49],
-        small[50],
-        small[51],
-        small[52],
-        small[53],
+        oimg.reshape(images.shape),
+        gimg.reshape(images.shape),
+        up,
+        gb.reshape(HID),
+        down,
+        dw,
+        r1,
+        r2,
+        r3,
+        r4,
+        r5,
     )
 
 

time: 278 us -> 239 us (0.86)
  Pallas kernels: 258 us -> 234 us
  local copies, waits for them, and re-layouts: 19.5 us -> 1.27 us
    pallas_call x1, Pallas kernels: 147 us -> 122 us  [second_call(): pl.pallas_call(second_kernel, out_shape=(jax.ShapeDtypeStruct((ROWS, CH),...]
    unnamed x12 -> x0, local copies, waits for them, and re-layouts: 11.5 us -> none
    pallas_call x0 -> x1, Pallas kernels: none -> 10.5 us  [last_call(): pl.pallas_call(last_kernel, out_shape=(wide, wide, jax.ShapeDtypeStruct((...]
    pallas_call x1, Pallas kernels: 111 us -> 102 us  [first_call(): pl.pallas_call(first_kernel, out_shape=(jax.ShapeDtypeStruct((ROWS, CH),...]
    slice x2 -> x0, local copies, waits for them, and re-layouts: 3.03 us -> none  [the longest x1 1.82 us: on_device(): small[53]]
where the time goes in v3:
time: 239 us; the launch traced here: 237 us
  Pallas kernels  234 us (98%)
    pallas_call x1, Pallas kernels, second_call(): pl.pallas_call(second_kernel, out_shape=(jax.ShapeDtypeStruct((ROWS, CH),...  122 us
    pallas_call x1, Pallas kernels, first_call(): pl.pallas_call(first_kernel, out_shape=(jax.ShapeDtypeStruct((ROWS, CH),...  102 us
    pallas_call x1, Pallas kernels, last_call(): pl.pallas_call(last_kernel, out_shape=(wide, wide, jax.ShapeDtypeStruct((...  10.5 us

profile of v3, /device:TPU:1, one launch (start us, length us, event | category | flops | bytes accessed | tf_op | source)
XLA Modules:
  0.0 237.3 jit_solution(8830716004607655367)
XLA Ops:
  0.6 1.3 reshape.63.bu
  1.9 101.8 %shard_map.194 = (f32[128,3072]{1,0:T(8,128)}, f32[128,128]{1,0:T(8,128)}, bf16[512,3072]{1,0:T(8,128)(2,1)}, bf16[512,3072]{1,0:T(8,128)(2,1)}, bf16[3072,768]{...) custom-call(bf16[128,3072]{1,0:T(8,128)(2,1)} %bitcast.9, ...), custom_call_target="tpu_custom_call" | custom-call | tf_op jit(solution)/shard_map/pallas_call | solution.py:447
  103.7 121.8 %shard_map.195 = (bf16[128,3072]{1,0:T(8,128)(2,1)}, bf16[128,3072]{1,0:T(8,128)(2,1)}, bf16[3072,768]{1,0:T(8,128)(2,1)}, bf16[768,3072]{1,0:T(8,128)(2,1)}, f32[64,3072]{1,0:T(8,128)}) custom-call(bf16[512,3072]{1,0:T(8,128)(2,1)} %get-tuple-element.37.pn, bf16[512,3072]{1,0:T(8,128)(2,1)} %get-tuple-element.38.pb, ...), custom_call_target="tpu_custom_call" | custom-call | tf_op jit(solution)/shard_map/pallas_call | solution.py:931
  225.5 10.5 %shard_map.196 = (bf16[128,3072]{1,0:T(8,128)(2,1)}, bf16[128,3072]{1,0:T(8,128)(2,1)}, bf16[3072,768]{1,0:T(8,128)(2,1)}, bf16[768,3072]{1,0:T(8,128)(2,1)}, f3...) custom-call(bf16[128,3072]{1,0:T(8,128)(2,1)} %get-tuple-element.47., ...), custom_call_target="tpu_custom_call" | custom-call | tf_op jit(solution)/shard_map/pallas_call | solution.py:991
  236.0 1.3 reduce

commit v4 on v3

--- a/solution.py
+++ b/solution.py
@@ -143,8 +143,8 @@
 
 def first_kernel(
     img, gout, dww, dwb, gain, shift, lscale, wu, wd, bu,
-    std, inv, pn, pb, keep_up, keep_down, got_up, got_down, bias_sums, scale_sums,
-    gn, gs, wuv, wdv, b_own, bo, hid, gp, keep32, pnv, pbv, up_v, down_v,
+    std, inv, hid_out, gp_out, gs_out, wu_out, wd_out, grad_up, grad_down, bias_sums,
+    gn, gs, wuv, wdv, b_own, bo, hid, gp, keep32, up_v, down_v,
     send, recv, local,
 ):
     me = Place()
@@ -155,7 +155,7 @@
     mate = me.at(core=me.other_core)
     wu_load = copies.here(wu, wuv.at[0])
     wd_load = copies.here(wd, wdv.at[0])
-    b_own[...] = jnp.broadcast_to(bu[...], (8, HID))
+    b_own[...] = jnp.broadcast_to(bu[...][None, :], (8, HID))
     z_right_chip, z_left_chip, z, z_right, z_left, z_far = me.ring("z")
     greet([right, left, cut, pair, mate, z_right_chip, z_left_chip])
 
@@ -318,59 +318,27 @@
 
         lax.fori_loop(0, HID // tile, body, 0)
 
-    keep = lax.rem(me.x_hi + me.core, 2)
-    moves = {}
-
-    def place(matrix, s, part):
+    outs = []
+
+    def part_place(matrix, s, part):
         if matrix == 0:
             at = (pl.ds(part * 768, 768), slice(None))
-            mine, there, ref = keep_up, got_up, up_v
+            outs.append(copies.here(up_v.at[(s,) + at], grad_up.at[(s,) + at]))
         else:
             at = (slice(None), pl.ds(part * 768, 768))
-            mine, there, ref = keep_down, got_down, down_v
-        if (matrix, part) not in moves:
-            index = copies.used_local
-            copies.used_local += 1
-            moves[matrix, part] = (
-                copies.remote(ref.at[at], there.at[at], mate),
-                pltpu.make_async_copy(ref.at[at], mine.at[at], local.at[index]),
-            )
-        away, stay = moves[matrix, part]
-
-        @pl.when(keep != s)
-        def _():
-            away.start()
-
-        @pl.when(keep == s)
-        def _():
-            stay.start()
-
-    def placed(matrix, s, part):
-        away, stay = moves[matrix, part]
-
-        @pl.when(keep != s)
-        def _():
-            away.wait_send()
-
-        @pl.when(keep == s)
-        def _():
-            stay.wait()
+            outs.append(copies.here(down_v.at[(s,) + at], grad_down.at[(s,) + at]))
 
     def part_up(s):
         for part in range(4):
-            if s == 1:
-                placed(0, 0, part)
             rows = pl.ds(part * 768, 768)
-            up_v[rows, :] = lax.dot_general(gn[:, rows], gp[s], TN, preferred_element_type=F32).astype(BF16)
-            place(0, s, part)
+            up_v[s, rows, :] = lax.dot_general(gn[:, rows], gp[s], TN, preferred_element_type=F32).astype(BF16)
+            part_place(0, s, part)
 
     def part_down(s):
         for part in range(4):
-            if s == 1:
-                placed(1, 0, part)
             cs = pl.ds(part * 768, 768)
-            down_v[:, cs] = lax.dot_general(hid[s], gs[:, cs], TN, preferred_element_type=F32).astype(BF16)
-            place(1, s, part)
+            down_v[s, :, cs] = lax.dot_general(hid[s], gs[:, cs], TN, preferred_element_type=F32).astype(BF16)
+            part_place(1, s, part)
 
     from_pair(0)
     from_ring(0, 0)
@@ -406,38 +374,15 @@
     part_up(0)
     part_down(1)
     arrived(1)
+    outs.append(copies.here(wuv.at[1], wu_out))
+    outs.append(copies.here(wdv.at[1], wd_out))
+    outs.append(copies.here(hid, hid_out))
+    outs.append(copies.here(gs, gs_out))
     other_grad()
+    outs.append(copies.here(gp, gp_out))
     part_up(1)
-    wide = 768
-
-    def normed_back(index, carry):
-        cs = pl.ds(pl.multiple_of(index * wide, wide), wide)
-        total = lax.dot_general(gp[0], wuv[0, cs, :], NT, preferred_element_type=F32)
-        total = total + lax.dot_general(gp[1], wuv[1, cs, :], NT, preferred_element_type=F32)
-        pnv[:, cs] = total.astype(BF16)
-        return carry
-
-    lax.fori_loop(0, CH // wide, normed_back, 0)
-    pn_out = copies.here(pnv, pn)
-
-    def branch_tile(index, carry):
-        cs = pl.ds(pl.multiple_of(index * wide, wide), wide)
-        total = jnp.dot(hid[0], wdv[0, :, cs], preferred_element_type=F32)
-        total = total + jnp.dot(hid[1], wdv[1, :, cs], preferred_element_type=F32)
-        pbv[:, cs] = total.astype(BF16)
-        product = jnp.sum(total * gs[:, cs].astype(F32), axis=0, keepdims=True)
-        scale_sums[0:1, cs] = product / lscale[0:1, cs]
-        return carry
-
-    lax.fori_loop(0, CH // wide, branch_tile, 0)
-    pb_out = copies.here(pbv, pb)
-
-    pn_out.wait()
-    pb_out.wait()
-    for matrix in range(2):
-        for part in range(4):
-            placed(matrix, 1, part)
-            moves[matrix, part][0].wait_recv()
+    for copy in outs:
+        copy.wait()
     copies.drain()
 
 
@@ -449,17 +394,17 @@
         out_shape=(
             jax.ShapeDtypeStruct((ROWS, CH), F32),
             jax.ShapeDtypeStruct((ROWS, LANES), F32),
-            jax.ShapeDtypeStruct((rows, CH), BF16),
+            jax.ShapeDtypeStruct((2, rows, HID), BF16),
+            jax.ShapeDtypeStruct((2, rows, HID), BF16),
             jax.ShapeDtypeStruct((rows, CH), BF16),
             jax.ShapeDtypeStruct((CH, HID), BF16),
             jax.ShapeDtypeStruct((HID, CH), BF16),
-            jax.ShapeDtypeStruct((CH, HID), BF16),
-            jax.ShapeDtypeStruct((HID, CH), BF16),
+            jax.ShapeDtypeStruct((2, CH, HID), BF16),
+            jax.ShapeDtypeStruct((2, HID, CH), BF16),
             jax.ShapeDtypeStruct((8, HID), F32),
-            jax.ShapeDtypeStruct((8, CH), F32),
         ),
         in_specs=[VMEM] * 7 + [ANY, ANY, VMEM],
-        out_specs=(VMEM, VMEM, ANY, ANY, ANY, ANY, ANY, ANY, VMEM, VMEM),
+        out_specs=(VMEM, VMEM, ANY, ANY, ANY, ANY, ANY, ANY, ANY, VMEM),
         scratch_shapes=[
             pltpu.VMEM((rows, CH), BF16),
             pltpu.VMEM((rows, CH), BF16),
@@ -470,13 +415,11 @@
             pltpu.VMEM((2, rows, HID), BF16),
             pltpu.VMEM((2, rows, HID), BF16),
             pltpu.VMEM((2, rows, HID), F32),
-            pltpu.VMEM((rows, CH), BF16),
-            pltpu.VMEM((rows, CH), BF16),
-            pltpu.VMEM((CH, HID), BF16),
-            pltpu.VMEM((HID, CH), BF16),
+            pltpu.VMEM((2, CH, HID), BF16),
+            pltpu.VMEM((2, HID, CH), BF16),
             pltpu.SemaphoreType.DMA((remote,)),
             pltpu.SemaphoreType.DMA((remote,)),
-            pltpu.SemaphoreType.DMA((12,)),
+            pltpu.SemaphoreType.DMA((32,)),
         ],
         compiler_params=pltpu.CompilerParams(
             collective_id=0, has_side_effects=True, vmem_limit_bytes=62 * 1024 * 1024
@@ -556,10 +499,10 @@
 
 
 def second_kernel(
-    pn, pb, gu, gd, ru, rd, img, gout, std, inv, dww, gain, lscale, bdown, pbias, pscale,
+    hid_in, gp_in, gs_in, wu, wd, wuo, wdo, gu, gd, img, gout, std, inv, dww, gain, lscale, bdown, pbias,
     out_img, grad_img, out_up, out_down, out_small,
     guv, gdv, cu, cd, d1a, d1b, u1a, u1b, d2a, d2b, u2a, u2b, tq, fd, fu,
-    nv, bv, n1, n2, b1, b2, gcv, sm, smc, sya, syb, sx, sz, smo,
+    nv, bv, n1, n2, b1, b2, hid, gp, wu_t, wd_t, gcv, sm, smc, sya, syb, sx, sz, smo,
     send, recv, local,
 ):
     me = Place()
@@ -574,33 +517,50 @@
     z_far, z_right, z_left = ring_z[5], ring_z[3], ring_z[4]
     x_far, x_right, x_left = ring_x[5], ring_x[3], ring_x[4]
     order = [(0, z_far), (1, x_far), (0, z_right), (1, x_right), (0, z_left), (1, x_left), (0, z), (1, x)]
+    keep = lax.rem(me.x_hi + me.core, 2)
+    give = 1 - keep
     swaps, loads = [], []
-    load_n = copies.here(pn, nv)
 
     def piece(matrix, which):
         return rows_at(which * 192, 192) if matrix == 0 else rows_at(which * 768, 768)
 
+    def fetch(index):
+        m, which = order[index]
+        src, mine = ((gd, gdv), (gu, guv))[m]
+        at = piece(m, which)
+        loads.append(copies.here(src.at[keep, at], mine.at[at]))
+
+    wide = 768
+
+    def up_tile(part):
+        at = pl.ds(part * wide, wide)
+        return [copies.here(ref.at[at], wu_t.at[part % 2, s]) for s, ref in enumerate((wu, wuo))]
+
+    def down_tile(part):
+        at = pl.ds(part * wide, wide)
+        return [copies.here(ref.at[:, at], wd_t.at[part % 2, s]) for s, ref in enumerate((wd, wdo))]
+
+    fetch(0)
+    fetch(1)
+    load_gp = copies.here(gp_in, gp)
+    tiles = {(0, 0): up_tile(0), (0, 1): up_tile(1)}
+    for index in range(2, 8):
+        fetch(index)
+    load_hid = copies.here(hid_in, hid)
+    load_gs = copies.here(gs_in, bv)
+    tiles[1, 0], tiles[1, 1] = down_tile(0), down_tile(1)
+    greet([ring_x[0], ring_x[1], ring_y[0], ring_y[1], ring_z[0], ring_z[1], mate])
     for m, which in order:
-        src, got, dst, mine = ((gd, rd, cd, gdv), (gu, ru, cu, guv))[m]
+        src, dst = ((gd, cd), (gu, cu))[m]
         at = piece(m, which)
-        swaps.append(copies.here(got.at[at], dst.at[at]))
-        loads.append(copies.here(src.at[at], mine.at[at]))
-    load_b = copies.here(pb, bv)
-    greet([ring_x[0], ring_x[1], ring_y[0], ring_y[1], ring_z[0], ring_z[1], mate])
-
-    y_far = ring_y[5]
-    load_n.wait()
-    rs_n = RingSum(copies, ring_y, nv, 0, ROWS, n2, n1)
-    rs_n.begin()
-    rs_n.own_halves()
-    rs_b = RingSum(copies, ring_y, bv, 0, ROWS, b2, b1)
+        swaps.append(copies.push(src.at[give, at], dst.at[at], mate))
 
     def merge(index):
         m, which = order[index]
         mine, other = ((gdv, cd), (guv, cu))[m]
         rows = 192 if m == 0 else 768
         loads[index].wait()
-        swaps[index].wait()
+        swaps[index].wait_recv()
         add_rows(mine, which * rows, [(other, which * rows, 0)], rows, 0, mine.shape[1], 16 if m == 0 else 64)
 
     rs_d1 = RingSum(copies, ring_z, gdv, 0, 192, d1b, d1a)
@@ -609,13 +569,41 @@
     rs_d1.begin()
     merge(1)
     rs_u1.begin()
+
+    load_gp.wait()
+    for part in range(4):
+        for copy in tiles[0, part]:
+            copy.wait()
+        slot = part % 2
+        total = lax.dot_general(gp[0], wu_t[slot, 0], NT, preferred_element_type=F32)
+        total = total + lax.dot_general(gp[1], wu_t[slot, 1], NT, preferred_element_type=F32)
+        nv[:, pl.ds(part * wide, wide)] = total.astype(BF16)
+        if part < 2:
+            tiles[0, part + 2] = up_tile(part + 2)
+    rs_n = RingSum(copies, ring_y, nv, 0, ROWS, n2, n1)
+    rs_n.begin()
+    rs_n.own_halves()
     for index in range(2, 6):
         merge(index)
     rs_d1.own_halves()
     rs_u1.own_halves()
-    load_b.wait()
+    load_hid.wait()
+    load_gs.wait()
+    for part in range(4):
+        for copy in tiles[1, part]:
+            copy.wait()
+        slot = part % 2
+        cs = pl.ds(part * wide, wide)
+        total = jnp.dot(hid[0], wd_t[slot, 0], preferred_element_type=F32)
+        total = total + jnp.dot(hid[1], wd_t[slot, 1], preferred_element_type=F32)
+        product = jnp.sum(total * bv[:, cs].astype(F32), axis=0, keepdims=True)
+        sm[53:54, cs] = product / lscale[0:1, cs]
+        bv[:, cs] = total.astype(BF16)
+        if part < 2:
+            tiles[1, part + 2] = down_tile(part + 2)
+    rs_b = RingSum(copies, ring_y, bv, 0, ROWS, b2, b1)
+    rs_n.middle()
     rs_b.begin()
-    rs_n.middle()
     rs_b.own_halves()
     rs_d1.middle()
     rs_u1.middle()
@@ -686,7 +674,7 @@
     def scale_block(block, carry):
         cs = lanes_at(block)
         upstream = jnp.sum(gout[:, cs].astype(F32), axis=0, keepdims=True)
-        sm[53:54, cs] = pscale[0:1, cs] + upstream * bdown[0:1, cs]
+        sm[53:54, cs] = sm[53:54, cs] + upstream * bdown[0:1, cs]
         return carry
 
     lax.fori_loop(0, BLOCKS, scale_block, 0)
@@ -774,7 +762,7 @@
     d_cut = copies.remote(fd, out_down.at[drow(x)], x_cut)
     d_swap = copies.remote(fd, out_down.at[drow(x)], x_pair)
     d_cut_swap = copies.remote(out_down.at[drow(me.x_cut)], out_down.at[drow(me.x_cut)], x_pair)
-    d_own = pltpu.make_async_copy(fd, out_down.at[drow(x)], local.at[30])
+    d_own = pltpu.make_async_copy(fd, out_down.at[drow(x)], local.at[62])
 
     @pl.when(jnp.logical_not(needed))
     def _():
@@ -847,7 +835,7 @@
     u_cut = copies.remote(tq, out_up.at[urow(x)], x_cut)
     u_swap = copies.remote(tq, out_up.at[urow(x)], x_pair)
     u_mate = copies.remote(tq, out_up.at[urow(x)], mate)
-    u_own = pltpu.make_async_copy(tq, out_up.at[urow(x)], local.at[31])
+    u_own = pltpu.make_async_copy(tq, out_up.at[urow(x)], local.at[63])
 
     @pl.when(jnp.logical_not(needed))
     def _():
@@ -925,7 +913,7 @@
 
 
 def second_call(*operands):
-    remote = 96
+    remote = 104
     bf = lambda *shape: pltpu.VMEM(shape, BF16)
     fl = lambda *shape: pltpu.VMEM(shape, F32)
     return pl.pallas_call(
@@ -937,7 +925,7 @@
             jax.ShapeDtypeStruct((HID, CH), BF16),
             jax.ShapeDtypeStruct((64, CH), F32),
         ),
-        in_specs=[ANY] * 6 + [VMEM] * 10,
+        in_specs=[ANY] * 9 + [VMEM] * 9,
         out_specs=(VMEM, VMEM, ANY, ANY, VMEM),
         scratch_shapes=[
             bf(CH, HID), bf(HID, CH), bf(CH, HID), bf(HID, CH),
@@ -946,14 +934,15 @@
             bf(768, 768), bf(48, 3072), bf(192, 768),
             bf(512, CH), bf(512, CH),
             bf(2, 128, 1536), bf(2, 128, 3072), bf(2, 128, 1536), bf(2, 128, 3072),
+            bf(2, 512, HID), bf(2, 512, HID), bf(2, 2, 768, HID), bf(2, 2, HID, 768),
             fl(ROWS, CH), fl(64, CH), fl(32, CH), fl(2, 8, 1536), fl(2, 8, CH),
             fl(4, 8, CH), fl(4, 8, CH), fl(64, CH),
             pltpu.SemaphoreType.DMA((remote,)),
             pltpu.SemaphoreType.DMA((remote,)),
-            pltpu.SemaphoreType.DMA((32,)),
+            pltpu.SemaphoreType.DMA((64,)),
         ],
         compiler_params=pltpu.CompilerParams(
-            collective_id=1, has_side_effects=True, vmem_limit_bytes=60 * 1024 * 1024
+            collective_id=1, has_side_effects=True, vmem_limit_bytes=63 * 1024 * 1024
         ),
     )(*operands)
 
@@ -1023,11 +1012,11 @@
     img = images.reshape(ROWS, CH)
     gout = grad_out.reshape(ROWS, CH)
     row = lambda vector: vector.reshape(1, CH)
-    std, inv, pn, pb, keep_up, keep_down, got_up, got_down, pbias, pscale = first_call(
-        img, gout, dw_weight, row(dw_bias), row(ln_gain), row(ln_bias), row(layer_scale), w_up, w_down, b_up.reshape(1, HID)
+    std, inv, hid, gp, gs, wuo, wdo, grad_up, grad_down, pbias = first_call(
+        img, gout, dw_weight, row(dw_bias), row(ln_gain), row(ln_bias), row(layer_scale), w_up, w_down, b_up
     )
     out_img, grad_img, out_up, out_down, small = second_call(
-        pn, pb, keep_up, keep_down, got_up, got_down, img, gout, std, inv, dw_weight, row(ln_gain), row(layer_scale), row(b_down), pbias, pscale
+        hid, gp, gs, w_up, w_down, wuo, wdo, grad_up, grad_down, img, gout, std, inv, dw_weight, row(ln_gain), row(layer_scale), row(b_down), pbias
     )
     oimg, gimg, up, down, dw, r1, r2, r3, r4, r5, gb = last_call(out_img, grad_img, out_up, out_down, small)
     return (

time: 239 us -> 227 us (0.950)
  Pallas kernels: 234 us -> 225 us
    pallas_call x1, Pallas kernels: 102 us -> 85 us  [first_call(): pl.pallas_call(first_kernel, out_shape=(jax.ShapeDtypeStruct((ROWS, CH),...]
    pallas_call x1, Pallas kernels: 122 us -> 129 us  [second_call(): pl.pallas_call(second_kernel, out_shape=(jax.ShapeDtypeStruct((ROWS, CH),...]
where the time goes in v4:
time: 227 us
  Pallas kernels  225 us (99%)
    pallas_call x1, Pallas kernels, second_call(): pl.pallas_call(second_kernel, out_shape=(jax.ShapeDtypeStruct((ROWS, CH),...  129 us
    pallas_call x1, Pallas kernels, first_call(): pl.pallas_call(first_kernel, out_shape=(jax.ShapeDtypeStruct((ROWS, CH),...  85 us
    pallas_call x1, Pallas kernels, last_call(): pl.pallas_call(last_kernel, out_shape=(wide, wide, jax.ShapeDtypeStruct((...  10.5 us

profile of v4, /device:TPU:1, one launch (start us, length us, event | category | flops | bytes accessed | tf_op | source)
XLA Modules:
  0.0 226.9 jit_solution(8180574572506236801)
XLA Ops:
  0.6 85.0 %shard_map.194 = (f32[128,3072]{1,0:T(8,128)}, f32[128,128]{1,0:T(8,128)}, bf16[2,512,768]{2,1,0:T(8,128)(2,1)}, bf16[2,512,768]{2,1,0:T(8,128)(2,1)}, bf16[512,...) custom-call(bf16[128,3072]{1,0:T(8,128)(2,1)} %bitcast.9, ...), custom_call_target="tpu_custom_call" | custom-call | tf_op jit(solution)/shard_map/pallas_call | solution.py:392
  85.7 129.4 %shard_map.195 = (bf16[128,3072]{1,0:T(8,128)(2,1)}, bf16[128,3072]{1,0:T(8,128)(2,1)}, bf16[3072,768]{1,0:T(8,128)(2,1)}, bf16[768,3072]{1,0:T(8,128)(2,1)}, f32[64,3072]{1,0:T(8,128)}) custom-call(bf16[2,512,768]{2,1,0:T(8,128)(2,1)} %get-tuple-element.37.hid_in, bf16[2,512,768]{2,1,0:T(8,128)(2,1)} %get-tuple-element.38.gp_in, ...), custom_call_target="tpu_custom_call" | custom-call | tf_op jit(solution)/shard_map/pallas_call | solution.py:919
  215.1 10.5 %shard_map.196 = (bf16[128,3072]{1,0:T(8,128)(2,1)}, bf16[128,3072]{1,0:T(8,128)(2,1)}, bf16[3072,768]{1,0:T(8,128)(2,1)}, bf16[768,3072]{1,0:T(8,128)(2,1)}, f3...) custom-call(bf16[128,3072]{1,0:T(8,128)(2,1)} %get-tuple-element.47., ...), custom_call_target="tpu_custom_call" | custom-call | tf_op jit(solution)/shard_map/pallas_call | solution.py:980
  225.6 1.3 reduce

commit v5 on v4

--- a/solution.py
+++ b/solution.py
@@ -349,9 +349,9 @@
     for copy in s_second + s_last:
         copy.wait_recv()
     own_grad_hidden()
+    n_last = forward(n_first, gn)
     from_ring(1, 0)
     from_ring(1, 1)
-    n_last = forward(n_first, gn)
     up_rows_of(0, y)
     from_far(0, 0)
     from_far(0, 1)
@@ -669,63 +669,7 @@
             grad_img[16 * r : 16 * r + 16, cs] = jnp.concatenate(sums[2 * r : 2 * r + 2], axis=0).astype(BF16)
         return carry
 
-    lax.fori_loop(0, BLOCKS, conv_back, 0)
-
-    def scale_block(block, carry):
-        cs = lanes_at(block)
-        upstream = jnp.sum(gout[:, cs].astype(F32), axis=0, keepdims=True)
-        sm[53:54, cs] = sm[53:54, cs] + upstream * bdown[0:1, cs]
-        return carry
-
-    lax.fori_loop(0, BLOCKS, scale_block, 0)
-    sm[54:64, :] = jnp.zeros((10, CH), F32)
-    for s in range(2):
-        shard = y * 2 + (me.x_hi if s == 0 else 1 - me.x_hi)
-        for line in range(2):
-
-            @pl.when(lax.div(shard, 4) == line)
-            def _(s=s, line=line):
-                at = pl.ds(pl.multiple_of(lax.rem(shard, 4) * HID, LANES), HID)
-                sm[54 + line : 55 + line, at] = pbias[s : s + 1, :]
-
-    swap_small = copies.push(sm.at[pl.ds(pl.multiple_of(me.other_core * 32, 8), 32)], smc, mate)
-    small_rows = me.core * 32
-    sm_at = pl.ds(pl.multiple_of(small_rows, 8), 32)
-    yr, yl, yy, y_right, y_left, y_far = ring_y
-    zr, zl = ring_z[0], ring_z[1]
-    h = CH // 2
-    lo, hi = pl.ds(0, h), pl.ds(h, h)
-
-    def small_piece(which):
-        return pl.ds(pl.multiple_of(small_rows + which * 8, 8), 8)
-
-    def all_begin(buffer, ring):
-        where = ring[2]
-        return [
-            copies.push(buffer.at[where], buffer.at[where], ring[0]),
-            copies.push(buffer.at[where], buffer.at[where], ring[1]),
-        ]
-
-    def all_middle(buffer, ring, one):
-        at_right, at_left = ring[3], ring[4]
-        one[0].wait_recv()
-        two = [copies.push(buffer.at[at_left, :, lo], buffer.at[at_left, :, lo], ring[0])]
-        one[1].wait_recv()
-        two.append(copies.push(buffer.at[at_right, :, hi], buffer.at[at_right, :, hi], ring[1]))
-        return two
-
-    def all_end(buffer, two):
-        for copy in two:
-            copy.wait_recv()
-        return buffer[0] + buffer[1] + buffer[2] + buffer[3]
-
-    rs_b.middle()
-    swap_small.wait_recv()
-    sm[sm_at, :] = sm[sm_at, :] + smc[...]
-    s_one = [
-        copies.push(sm.at[small_piece(y_far), lo], sya.at[0], yr),
-        copies.push(sm.at[small_piece(y_far), hi], sya.at[1], yl),
-    ]
+    lax.fori_loop(0, BLOCKS // 2, conv_back, 0)
 
     rs_d1.end()
     rs_d2 = RingSum(copies, ring_x, gdv, z * 192, 48, d2b, d2a)
@@ -735,6 +679,126 @@
     rs_u2 = RingSum(copies, ring_z, guv, x * 768, 192, u2b, u2a)
     rs_u2.begin()
     rs_u2.own_halves()
+    lax.fori_loop(BLOCKS // 2, BLOCKS, conv_back, 0)
+
+    def scale_block(block, carry):
+        cs = lanes_at(block)
+        upstream = jnp.sum(gout[:, cs].astype(F32), axis=0, keepdims=True)
+        sm[53:54, cs] = sm[53:54, cs] + upstream * bdown[0:1, cs]
+        return carry
+
+    lax.fori_loop(0, BLOCKS, scale_block, 0)
+    sm[54:64, :] = jnp.zeros((10, CH), F32)
+    for s in range(2):
+        shard = y * 2 + (me.x_hi if s == 0 else 1 - me.x_hi)
+        for line in range(2):
+
+            @pl.when(lax.div(shard, 4) == line)
+            def _(s=s, line=line):
+                at = pl.ds(pl.multiple_of(lax.rem(shard, 4) * HID, LANES), HID)
+                sm[54 + line : 55 + line, at] = pbias[s : s + 1, :]
+
+    swap_small = copies.push(sm.at[pl.ds(pl.multiple_of(me.other_core * 32, 8), 32)], smc, mate)
+    small_rows = me.core * 32
+    sm_at = pl.ds(pl.multiple_of(small_rows, 8), 32)
+    yr, yl, yy, y_right, y_left, y_far = ring_y
+    zr, zl = ring_z[0], ring_z[1]
+    h = CH // 2
+    lo, hi = pl.ds(0, h), pl.ds(h, h)
+
+    def small_piece(which):
+        return pl.ds(pl.multiple_of(small_rows + which * 8, 8), 8)
+
+    def all_begin(buffer, ring):
+        where = ring[2]
+        return [
+            copies.push(buffer.at[where], buffer.at[where], ring[0]),
+            copies.push(buffer.at[where], buffer.at[where], ring[1]),
+        ]
+
+    def all_middle(buffer, ring, one):
+        at_right, at_left = ring[3], ring[4]
+        one[0].wait_recv()
+        two = [copies.push(buffer.at[at_left, :, lo], buffer.at[at_left, :, lo], ring[0])]
+        one[1].wait_recv()
+        two.append(copies.push(buffer.at[at_right, :, hi], buffer.at[at_right, :, hi], ring[1]))
+        return two
+
+    def all_end(buffer, two):
+        for copy in two:
+            copy.wait_recv()
+        return buffer[0] + buffer[1] + buffer[2] + buffer[3]
+
+    rs_d2.middle()
+    rs_u2.middle()
+    swap_small.wait_recv()
+    sm[sm_at, :] = sm[sm_at, :] + smc[...]
+    s_one = [
+        copies.push(sm.at[small_piece(y_far), lo], sya.at[0], yr),
+        copies.push(sm.at[small_piece(y_far), hi], sya.at[1], yl),
+    ]
+    rs_b.middle()
+
+    rs_d2.end()
+    at_d = z * 192 + x * 48
+    at_u = x * 768 + z * 192
+    fd[...] = (gdv[rows_at(at_d, 48), :].astype(F32) * factor).astype(BF16)
+    needed = me.x_hi == me.core
+
+    def drow(which_x):
+        return rows_at(z * 192 + which_x * 48, 48)
+
+    d_cut = copies.remote(fd, out_down.at[drow(x)], x_cut)
+    d_swap = copies.remote(fd, out_down.at[drow(x)], x_pair)
+    d_cut_swap = copies.remote(out_down.at[drow(me.x_cut)], out_down.at[drow(me.x_cut)], x_pair)
+    d_own = pltpu.make_async_copy(fd, out_down.at[drow(x)], local.at[62])
+
+    @pl.when(jnp.logical_not(needed))
+    def _():
+        d_cut.start()
+
+    @pl.when(needed)
+    def _():
+        d_own.start()
+        d_swap.start()
+
+    rs_u2.end()
+    fu[...] = (guv[rows_at(at_u, 192), :].astype(F32) * factor).astype(BF16)
+
+    def slot(which):
+        return rows_at(which * 192, 192)
+
+    def upiece(which_x, which):
+        return rows_at(which_x * 768 + which * 192, 192)
+
+    spots = (z, z_left, z_right, z_far)
+    u_cut, u_swap, u_cut_swap = [], [], []
+    for index, spot in enumerate(spots):
+        piece_ref = fu if index == 0 else tq.at[slot(spot)]
+        u_cut.append(copies.remote(piece_ref, out_up.at[upiece(x, spot)], x_cut))
+        u_swap.append(copies.remote(piece_ref, out_up.at[upiece(x, spot)], x_pair))
+        far_ref = out_up.at[upiece(me.x_cut, spot)]
+        u_cut_swap.append(copies.remote(far_ref, far_ref, x_pair))
+
+    def start_up(index):
+        @pl.when(jnp.logical_not(needed))
+        def _():
+            u_cut[index].start()
+
+        @pl.when(needed)
+        def _():
+            u_swap[index].start()
+
+    def cross_up(*indices):
+        @pl.when(needed)
+        def _():
+            for index in indices:
+                u_cut[index].wait_recv()
+                u_cut_swap[index].start()
+
+    tq_own = copies.here(fu, tq.at[slot(z)])
+    up_one = [copies.push(fu, tq.at[slot(z)], zr), copies.push(fu, tq.at[slot(z)], zl)]
+    start_up(0)
 
     s_two = []
     for side, (device, which) in enumerate(((yr, y_right), (yl, y_left))):
@@ -742,70 +806,26 @@
         at = small_piece(which)
         sm[at, pl.ds(side * h, h)] = sm[at, pl.ds(side * h, h)] + sya[side]
         s_two.append(copies.push(sm.at[at], syb.at[side], device))
-    rs_d2.middle()
-    rs_u2.middle()
-    for side in range(2):
-        s_two[side].wait_recv()
-    at = small_piece(yy)
-    sx[pl.ds(x, 1)] = (sm[at, :] + syb[0] + syb[1])[None]
-    sx_one = all_begin(sx, ring_x)
-
-    rs_d2.end()
-    at_d = z * 192 + x * 48
-    at_u = x * 768 + z * 192
-    fd[...] = (gdv[rows_at(at_d, 48), :].astype(F32) * factor).astype(BF16)
-    needed = me.x_hi == me.core
-
-    def drow(which_x):
-        return rows_at(z * 192 + which_x * 48, 48)
-
-    d_cut = copies.remote(fd, out_down.at[drow(x)], x_cut)
-    d_swap = copies.remote(fd, out_down.at[drow(x)], x_pair)
-    d_cut_swap = copies.remote(out_down.at[drow(me.x_cut)], out_down.at[drow(me.x_cut)], x_pair)
-    d_own = pltpu.make_async_copy(fd, out_down.at[drow(x)], local.at[62])
-
-    @pl.when(jnp.logical_not(needed))
-    def _():
-        d_cut.start()
-
-    @pl.when(needed)
-    def _():
-        d_own.start()
-        d_swap.start()
-
-    rs_u2.end()
-    fu[...] = (guv[rows_at(at_u, 192), :].astype(F32) * factor).astype(BF16)
-
-    def slot(which):
-        return rows_at(which * 192, 192)
-
-    tq_own = copies.here(fu, tq.at[slot(z)])
-    up_one = [copies.push(fu, tq.at[slot(z)], zr), copies.push(fu, tq.at[slot(z)], zl)]
-    sx_two = all_middle(sx, ring_x, sx_one)
-
-    rs_b.end()
-
-    def result_block(block, carry):
-        cs = lanes_at(block)
-        branch = own_rows(bv, cs) + bdown[0:1, cs]
-        out_img[:, cs] = (img[:, cs].astype(F32) + lscale[0:1, cs] * branch).astype(BF16)
-        return carry
-
-    lax.fori_loop(0, BLOCKS, result_block, 0)
 
     @pl.when(needed)
     def _():
         d_cut.wait_recv()
         d_cut_swap.start()
 
-    sz[pl.ds(z, 1)] = all_end(sx, sx_two)[None]
+    for side in range(2):
+        s_two[side].wait_recv()
+    at = small_piece(yy)
+    sz[pl.ds(z, 1)] = (sm[at, :] + syb[0] + syb[1])[None]
     sz_one = all_begin(sz, ring_z)
+
     hu = HID // 2
     z_left_slot, z_right_slot = slot(z_left), slot(z_right)
     up_one[0].wait_recv()
     up_two = [copies.push(tq.at[z_left_slot, pl.ds(0, hu)], tq.at[z_left_slot, pl.ds(0, hu)], zr)]
+    start_up(1)
     up_one[1].wait_recv()
     up_two.append(copies.push(tq.at[z_right_slot, pl.ds(hu, hu)], tq.at[z_right_slot, pl.ds(hu, hu)], zl))
+    start_up(2)
     sz_two = all_middle(sz, ring_z, sz_one)
 
     def dblock(which):
@@ -827,27 +847,38 @@
 
     for copy in up_two:
         copy.wait_recv()
+    start_up(3)
+    cross_up(0)
     tq_own.wait()
 
     def urow(which_x):
         return rows_at(which_x * 768, 768)
 
-    u_cut = copies.remote(tq, out_up.at[urow(x)], x_cut)
-    u_swap = copies.remote(tq, out_up.at[urow(x)], x_pair)
     u_mate = copies.remote(tq, out_up.at[urow(x)], mate)
     u_own = pltpu.make_async_copy(tq, out_up.at[urow(x)], local.at[63])
 
-    @pl.when(jnp.logical_not(needed))
-    def _():
-        u_cut.start()
-
     @pl.when(needed)
     def _():
-        u_swap.start()
         u_mate.start()
         u_own.start()
 
-    total = all_end(sz, sz_two)
+    sx[pl.ds(x, 1)] = all_end(sz, sz_two)[None]
+    sx_one = all_begin(sx, ring_x)
+    cross_up(1)
+
+    rs_b.end()
+
+    def result_block(block, carry):
+        cs = lanes_at(block)
+        branch = own_rows(bv, cs) + bdown[0:1, cs]
+        out_img[:, cs] = (img[:, cs].astype(F32) + lscale[0:1, cs] * branch).astype(BF16)
+        return carry
+
+    lax.fori_loop(0, BLOCKS, result_block, 0)
+    sx_two = all_middle(sx, ring_x, sx_one)
+    cross_up(2)
+
+    total = all_end(sx, sx_two)
     smo_at = small_piece(yy)
     smo[smo_at, :] = total * factor
     so_one = [
@@ -855,6 +886,7 @@
         copies.push(smo.at[smo_at], smo.at[smo_at], yl),
     ]
     from_left, from_right = small_piece(y_left), small_piece(y_right)
+    cross_up(3)
     so_one[0].wait_recv()
     so_two = [copies.push(smo.at[from_left, lo], smo.at[from_left, lo], yr)]
     so_one[1].wait_recv()
@@ -869,16 +901,16 @@
     d_mate_l = copies.remote(out_down.at[block_l], out_down.at[block_l], mate)
     d_mate_r = copies.remote(out_down.at[block_r], out_down.at[block_r], mate)
     d_mate_f = copies.remote(out_down.at[block_f], out_down.at[block_f], mate)
-    q_cut, q_pair, q_far = urow(me.x_cut), urow(me.x_pair), urow(3 - me.x_pair)
-    u_cut_swap = copies.remote(out_up.at[q_cut], out_up.at[q_cut], x_pair)
+    q_cut, q_pair = urow(me.x_cut), urow(me.x_pair)
     u_mate_c = copies.remote(out_up.at[q_cut], out_up.at[q_cut], mate)
     u_mate_p = copies.remote(out_up.at[q_pair], out_up.at[q_pair], mate)
-    u_mate_f = copies.remote(out_up.at[q_far], out_up.at[q_far], mate)
+    u_mate_f = []
+    for spot in spots:
+        far_ref = out_up.at[upiece(3 - me.x_pair, spot)]
+        u_mate_f.append(copies.remote(far_ref, far_ref, mate))
 
     @pl.when(needed)
     def _():
-        u_cut.wait_recv()
-        u_cut_swap.start()
         u_mate_c.start()
         d_right.wait_recv()
         d_fwd_right.start()
@@ -886,26 +918,31 @@
         d_left.wait_recv()
         d_fwd_left.start()
         d_mate_r.start()
-        u_swap.wait_recv()
+        for copy in u_swap:
+            copy.wait_recv()
         u_mate_p.start()
+        for index in range(3):
+            u_cut_swap[index].wait_recv()
+            u_mate_f[index].start()
         d_fwd_right.wait_recv()
         d_fwd_left.wait_recv()
         d_mate_f.start()
-        u_cut_swap.wait_recv()
-        u_mate_f.start()
+        u_cut_swap[3].wait_recv()
+        u_mate_f[3].start()
         u_own.wait()
         for copy in (
             d_swap, d_cut_swap, d_right, d_left, d_mate, d_fwd_right, d_fwd_left, d_mate_l, d_mate_r, d_mate_f,
-            u_swap, u_mate, u_cut_swap, u_mate_c, u_mate_p, u_mate_f,
+            u_mate, u_mate_c, u_mate_p, *u_swap, *u_cut_swap, *u_mate_f,
         ):
             copy.wait_send()
 
     @pl.when(jnp.logical_not(needed))
     def _():
-        for copy in (d_mate, d_mate_l, d_mate_r, d_mate_f, u_mate, u_mate_c, u_mate_p, u_mate_f):
+        for copy in (d_mate, d_mate_l, d_mate_r, d_mate_f, u_mate, u_mate_c, u_mate_p, *u_mate_f):
             copy.wait_recv()
         d_cut.wait_send()
-        u_cut.wait_send()
+        for copy in u_cut:
+            copy.wait_send()
 
     small_mate.wait_recv()
     out_small[...] = smo[...]
@@ -913,7 +950,7 @@
 
 
 def second_call(*operands):
-    remote = 104
+    remote = 128
     bf = lambda *shape: pltpu.VMEM(shape, BF16)
     fl = lambda *shape: pltpu.VMEM(shape, F32)
     return pl.pallas_call(

time: 227 us -> 221 us (0.974)
  Pallas kernels: 225 us -> 218 us
    pallas_call x1, Pallas kernels: 129 us -> 123 us  [second_call(): pl.pallas_call(second_kernel, out_shape=(jax.ShapeDtypeStruct((ROWS, CH),...]
where the time goes in v5:
time: 221 us; the launch traced here: 220 us
  Pallas kernels  218 us (99%)
    pallas_call x1, Pallas kernels, second_call(): pl.pallas_call(second_kernel, out_shape=(jax.ShapeDtypeStruct((ROWS, CH),...  123 us
    pallas_call x1, Pallas kernels, first_call(): pl.pallas_call(first_kernel, out_shape=(jax.ShapeDtypeStruct((ROWS, CH),...  85 us
    pallas_call x1, Pallas kernels, last_call(): pl.pallas_call(last_kernel, out_shape=(wide, wide, jax.ShapeDtypeStruct((...  10.5 us

profile of v5, /device:TPU:1, one launch (start us, length us, event | category | flops | bytes accessed | tf_op | source)
XLA Modules:
  0.0 220.4 jit_solution(16982546460343819477)
XLA Ops:
  0.6 85.0 %shard_map.194 = (f32[128,3072]{1,0:T(8,128)}, f32[128,128]{1,0:T(8,128)}, bf16[2,512,768]{2,1,0:T(8,128)(2,1)}, bf16[2,512,768]{2,1,0:T(8,128)(2,1)}, bf16[512,...) custom-call(bf16[128,3072]{1,0:T(8,128)(2,1)} %bitcast.9, ...), custom_call_target="tpu_custom_call" | custom-call | tf_op jit(solution)/shard_map/pallas_call | solution.py:392
  85.7 123.0 %shard_map.195 = (bf16[128,3072]{1,0:T(8,128)(2,1)}, bf16[128,3072]{1,0:T(8,128)(2,1)}, bf16[3072,768]{1,0:T(8,128)(2,1)}, bf16[768,3072]{1,0:T(8,128)(2,1)}, f32[64,3072]{1,0:T(8,128)}) custom-call(bf16[2,512,768]{2,1,0:T(8,128)(2,1)} %get-tuple-element.37.hid_in, bf16[2,512,768]{2,1,0:T(8,128)(2,1)} %get-tuple-element.38.gp_in, ...), custom_call_target="tpu_custom_call" | custom-call | tf_op jit(solution)/shard_map/pallas_call | solution.py:956
  208.7 10.5 %shard_map.196 = (bf16[128,3072]{1,0:T(8,128)(2,1)}, bf16[128,3072]{1,0:T(8,128)(2,1)}, bf16[3072,768]{1,0:T(8,128)(2,1)}, bf16[768,3072]{1,0:T(8,128)(2,1)}, f3...) custom-call(bf16[128,3072]{1,0:T(8,128)(2,1)} %get-tuple-element.47., ...), custom_call_target="tpu_custom_call" | custom-call | tf_op jit(solution)/shard_map/pallas_call | solution.py:1017
  219.2 1.3 reduce

commit v6 on v5

--- a/solution.py
+++ b/solution.py
@@ -348,6 +348,7 @@
     wd_load.wait()
     for copy in s_second + s_last:
         copy.wait_recv()
+    outs.append(copies.here(gs, gs_out))
     own_grad_hidden()
     n_last = forward(n_first, gn)
     from_ring(1, 0)
@@ -363,6 +364,7 @@
     from_far(1, 0)
     from_far(1, 1)
     arrived(0)
+    outs.append(copies.here(wuv.at[1], wu_out))
     up_rows_of(1, y)
     up_rows_of(1, y_right)
     up_rows_of(1, y_left)
@@ -370,14 +372,12 @@
         copy.wait_recv()
     up_rows_of(0, y_far)
     up_rows_of(1, y_far)
+    outs.append(copies.here(hid, hid_out))
     part_down(0)
     part_up(0)
     part_down(1)
     arrived(1)
-    outs.append(copies.here(wuv.at[1], wu_out))
     outs.append(copies.here(wdv.at[1], wd_out))
-    outs.append(copies.here(hid, hid_out))
-    outs.append(copies.here(gs, gs_out))
     other_grad()
     outs.append(copies.here(gp, gp_out))
     part_up(1)
@@ -1003,7 +1003,7 @@
     shard = lax.axis_index("fsdp")
     at = pl.ds(pl.multiple_of(lax.rem(shard, 4) * HID, LANES), HID)
     line = lax.div(shard, 4)
-    gb[...] = jnp.where(line == 0, small[54:55, at], small[55:56, at]).astype(BF16)
+    gb[...] = jnp.where(line == 0, small[54, at], small[55, at]).astype(BF16)
     for first, second in zip(loads, stores):
         first.wait()
         second.start()
@@ -1027,7 +1027,7 @@
             line,
             line,
             line,
-            jax.ShapeDtypeStruct((1, HID), BF16),
+            jax.ShapeDtypeStruct((HID,), BF16),
         ),
         in_specs=[ANY] * 4 + [VMEM],
         out_specs=tuple([ANY] * 4 + [VMEM] * 7),
@@ -1060,7 +1060,7 @@
         oimg.reshape(images.shape),
         gimg.reshape(images.shape),
         up,
-        gb.reshape(HID),
+        gb,
         down,
         dw,
         r1,

time: 221 us -> 219 us (level)
  no operation moved by 1% of the time
where the time goes in v6:
time: 219 us
  Pallas kernels  218 us (100%)
    pallas_call x1, Pallas kernels, second_call(): pl.pallas_call(second_kernel, out_shape=(jax.ShapeDtypeStruct((ROWS, CH),...  123 us
    pallas_call x1, Pallas kernels, first_call(): pl.pallas_call(first_kernel, out_shape=(jax.ShapeDtypeStruct((ROWS, CH),...  84.6 us
    pallas_call x1, Pallas kernels, last_call(): pl.pallas_call(last_kernel, out_shape=(wide, wide, jax.ShapeDtypeStruct((...  10.5 us

profile of v6, /device:TPU:1, one launch (start us, length us, event | category | flops | bytes accessed | tf_op | source)
XLA Modules:
  0.0 218.6 jit_solution(7280920475858224814)
XLA Ops:
  0.6 84.6 %shard_map.194 = (f32[128,3072]{1,0:T(8,128)}, f32[128,128]{1,0:T(8,128)}, bf16[2,512,768]{2,1,0:T(8,128)(2,1)}, bf16[2,512,768]{2,1,0:T(8,128)(2,1)}, bf16[512,...) custom-call(bf16[128,3072]{1,0:T(8,128)(2,1)} %bitcast.9, ...), custom_call_target="tpu_custom_call" | custom-call | tf_op jit(solution)/shard_map/pallas_call | solution.py:392
  85.3 122.7 %shard_map.195 = (bf16[128,3072]{1,0:T(8,128)(2,1)}, bf16[128,3072]{1,0:T(8,128)(2,1)}, bf16[3072,768]{1,0:T(8,128)(2,1)}, bf16[768,3072]{1,0:T(8,128)(2,1)}, f32[64,3072]{1,0:T(8,128)}) custom-call(bf16[2,512,768]{2,1,0:T(8,128)(2,1)} %get-tuple-element.37.hid_in, bf16[2,512,768]{2,1,0:T(8,128)(2,1)} %get-tuple-element.38.gp_in, ...), custom_call_target="tpu_custom_call" | custom-call | tf_op jit(solution)/shard_map/pallas_call | solution.py:956
  208.0 10.5 %shard_map.196 = (bf16[128,3072]{1,0:T(8,128)(2,1)}, bf16[128,3072]{1,0:T(8,128)(2,1)}, bf16[3072,768]{1,0:T(8,128)(2,1)}, bf16[768,3072]{1,0:T(8,128)(2,1)}, f3...) custom-call(bf16[128,3072]{1,0:T(8,128)(2,1)} %get-tuple-element.47., ...), custom_call_target="tpu_custom_call" | custom-call | tf_op jit(solution)/shard_map/pallas_call | solution.py:1017
